TPU v7x, 256 devices: a whole 4x4x8 slice. The times are simulated.
256 devices in a mesh: row: 32 (over y, z_hi, core), col: 8 (over z_lo, x).
Axes of the slice: x: 4, y: 4, z: 8 (z_hi: 4, z_lo: 2; z = z_hi * 2 + z_lo), core: 2. Of those that a mesh axis runs over, the one named last changes fastest.
Arguments:
- src_pos: float32 [128, 65536], P('col', 'row'), may hold values from -1 to 1
- tgt_pos: float32 [128, 16384], P('row', 'col'), may hold values from -1 to 1
- coupling: bfloat16 [65536, 16384], P('row', 'col'), may hold values from 0 to 36, as said below
- prior_tgt: float32 [16384], P('col'), may hold values from -4 to 4
Outputs:
- src_potential: float32 [65536], P('row')
- tgt_potential: float32 [16384], P('col')
Inputs may be any that keep to these rules, and one draw needn't show every extreme that they name: `coupling`: all entries are positive.
All inputs are finite; a program needn't handle non-finite values.
Results may differ from a plain program's by a relative error of at most 0.0003.
Values sent between devices are 32-bit elements; how exact they have to be, the bound alone decides.
A program may use at most 128 MiB of HBM per device.

v0:
```python
import math

import jax
import jax.numpy as jnp
from jax import lax
from jax.sharding import PartitionSpec as P

SWEEPS = 2


EPSILON = 0.25


def factors(positions):
    squared = jnp.sum(positions * positions, axis=0, keepdims=True)
    unit_row = jnp.ones_like(squared)
    left_side = jnp.concatenate([positions, squared, unit_row], axis=0)
    right_side = jnp.concatenate([-2.0 * positions, unit_row, squared], axis=0)
    return (left_side, right_side.astype(jnp.bfloat16))


def across_targets(values):
    highest = jnp.max(values, axis=1)
    highest = lax.pmax(highest, "col")
    summed = lax.psum(jnp.sum(jnp.exp(values - highest[:, None]), axis=1), "col")
    return highest + jnp.log(summed)


def across_sources(values):
    highest = jnp.max(values, axis=0)
    highest = lax.pmax(highest, "row")
    summed = lax.psum(jnp.sum(jnp.exp(values - highest[None, :]), axis=0), "row")
    return highest + jnp.log(summed)


def local(src_pos, tgt_pos, coupling, prior_tgt):
    src_full = lax.all_gather(src_pos, "col", axis=0, tiled=True)
    tgt_full = lax.all_gather(tgt_pos, "row", axis=0, tiled=True)
    rows_here, cols_here = coupling.shape
    total_src = rows_here * lax.axis_size("row")
    total_tgt = cols_here * lax.axis_size("col")
    src_left, src_right = factors(src_full)
    tgt_left, tgt_right = factors(tgt_full)
    tgt_right_wide = tgt_right.astype(jnp.float32)
    panel_sum = jnp.dot(src_right, coupling, preferred_element_type=jnp.float32)
    contract_dims = (((1,), (1,)), ((), ()))
    panel_sum = lax.psum(panel_sum, "row")
    core_part = lax.dot_general(
        panel_sum, tgt_right_wide, contract_dims, precision=lax.Precision.HIGHEST
    )
    core_matrix = lax.psum(core_part, "col")
    core_matrix = core_matrix / (total_src * total_tgt)
    rows_core = lax.dot_general(
        src_left, core_matrix, (((0,), (0,)), ((), ())), precision=lax.Precision.HIGHEST
    )
    cost_tile = -2.0 * jnp.dot(rows_core, tgt_left, precision=lax.Precision.HIGHEST)
    shift_src = -EPSILON * math.log(total_src)
    shift_tgt = -EPSILON * math.log(total_tgt)
    target_pot = prior_tgt
    source_pot = jnp.zeros((rows_here,), jnp.float32)
    for repeat in range(SWEEPS):
        source_pot = shift_src - EPSILON * across_targets(
            (target_pot[None, :] - cost_tile) / EPSILON
        )
        target_pot = shift_tgt - EPSILON * across_sources(
            (source_pot[:, None] - cost_tile) / EPSILON
        )
    return (source_pot, target_pot)


def solution(mesh):
    placed = (P("col", "row"), P("row", "col"), P("row", "col"), P("col"))
    return jax.shard_map(
        local, mesh=mesh, in_specs=placed, out_specs=(P("row"), P("col")), check_vma=False
    )
```

profile of v0, /device:TPU:1, one launch (start us, length us, event | category | flops | bytes accessed | tf_op | source)
XLA Modules:
  0.0 904.7 jit_solution(11925522181712462492)
XLA Ops:
  7.2 0.0 copy-start.2
  7.2 0.0 all-gather.4.cloned.1.call-start
  7.2 0.7 all-gather.4.cloned.1.call-update
  7.9 0.0 all-gather.6.cloned.1.call-start
  8.0 0.7 all-gather.6.cloned.1.call-update
  8.7 0.0 all-reduce.3.cloned.1.call-start
  8.7 41.4 %all-gather.4.cloned.1.call-done = f32[128,2048]{1,0:T(8,128)} async-done(((f32[16,2048]{1,0:T(8,128)}), f32[128,2048]{1,0:T(8,128)}) %all-gather.4.cloned.1.call-update) | async-done | bytes 1048592 | tf_op jit(solution)/shard_map/all_gather | solution.py:37
  50.1 0.0 copy-start
  50.1 1.5 multiply_convert_fusion.1
  51.6 5.8 fusion.16
  57.4 0.0 all-reduce.3.cloned.1.call-update
  57.4 0.0 all-reduce.5.cloned.1.call-start
  57.5 51.8 %all-gather.6.cloned.1.call-done = f32[32,4,2048]{2,1,0:T(4,128)} async-done(((f32[1,4,2048]{2,1,0:T(4,128)}), f32[32,4,2048]{2,1,0:T(4,128)}) %all-gather.6.cloned.1.call-update) | async-done | bytes 1048592 | tf_op jit(solution)/shard_map/all_gather | solution.py:38
  109.3 1.6 reshape.13
  110.9 0.1 multiply_convert_fusion
  111.1 276.8 %all-reduce.3.cloned.1.call-done = f32[130,2048]{1,0:T(8,128)} async-done(((f32[130,2048]{1,0:T(8,128)}), f32[130,2048]{1,0:T(8,128)}) %all-reduce.3.cloned.1.call-update) | async-done | bytes 1064976 | tf_op jit(solution)/shard_map/psum | solution.py:47
  387.9 2.7 fusion.21
  390.6 0.0 all-reduce.5.cloned.1.call-update
  390.6 0.1 pad.11.clone
  390.7 69.3 %all-reduce.5.cloned.1.call-done = f32[130,130]{1,0:T(8,128)} async-done(((f32[130,130]{1,0:T(8,128)}), f32[130,130]{1,0:T(8,128)}) %all-reduce.5.cloned.1.call-update) | async-done | bytes 67616 | tf_op jit(solution)/shard_map/psum | solution.py:51
  460.0 0.0 copy-done
  460.0 4.6 fusion.4
  464.6 0.0 copy-done.2
  464.6 18.2 %fusion = (f32[2048]{0:T(1024)S(1)}, f32[2048,2048]{1,0:T(8,128)}) fusion(f32[2048]{0:T(1024)S(1)} %copy-done.2, f32[2048,130]{1,0:T(8,128)S(1)} %fusion.4, f32[1,2048]{1,0:T(1,128)S(1)} %bitcast.11, f32[128,2048]{1,0:T(8,128)S(1)} %reshape.13, f32[130]{0:T(256)S(1)} %pad.11.clone), kind=kOutput, calls=%fused_computation.8 | convolution fusion | flops 6560421888 | bytes 18915848 | tf_op jit(solution)/shard_map/dot_general | solution.py:56
  482.8 13.3 %pmax.28 = f32[2048]{0:T(1024)S(1)} all-reduce(f32[2048]{0:T(1024)S(1)} %get-tuple-element.6), channel_id=1, replica_groups=mesh['row'=32,'col'=8] {'col'}, use_global_device_ids=true, to_apply=%region_5.0 | all-reduce | flops 2048 | bytes 16384 | tf_op jit(solution)/shard_map/pmax | solution.py:24
  496.1 8.2 exponential_reduce_fusion.3
  504.4 13.7 %psum.44 = f32[2048]{0:T(1024)S(1)} all-reduce(f32[2048]{0:T(1024)S(1)} %exponential_reduce_fusion.3), channel_id=1, replica_groups=mesh['row'=32,'col'=8] {'col'}, use_global_device_ids=true, to_apply=%region_7.0 | all-reduce | flops 2048 | bytes 16384 | tf_op jit(solution)/shard_map/psum | solution.py:25
  518.1 8.0 fusion.1
  526.1 83.7 %pmax.29 = f32[2048]{0:T(1024)S(1)} all-reduce(f32[2048]{0:T(1024)S(1)} %fusion.1), channel_id=1, replica_groups=mesh['row'=32,'col'=8] {'row'}, use_global_device_ids=true, to_apply=%region_9.0 | all-reduce | flops 2048 | bytes 16384 | tf_op jit(solution)/shard_map/pmax | solution.py:31
  609.9 8.2 exponential_reduce_fusion.2
  618.1 70.6 %psum.45 = f32[2048]{0:T(1024)S(1)} all-reduce(f32[2048]{0:T(1024)S(1)} %exponential_reduce_fusion.2), channel_id=1, replica_groups=mesh['row'=32,'col'=8] {'row'}, use_global_device_ids=true, to_apply=%region_11.0 | all-reduce | flops 2048 | bytes 16384 | tf_op jit(solution)/shard_map/psum | solution.py:32
  688.7 8.0 fusion.2
  696.7 12.7 %pmax.30 = f32[2048]{0:T(1024)S(1)} all-reduce(f32[2048]{0:T(1024)S(1)} %fusion.2), channel_id=1, replica_groups=mesh['row'=32,'col'=8] {'col'}, use_global_device_ids=true, to_apply=%region_13.0 | all-reduce | flops 2048 | bytes 16384 | tf_op jit(solution)/shard_map/pmax | solution.py:24
  709.5 8.2 exponential_reduce_fusion.1
  717.7 14.8 %psum.46 = f32[2048]{0:T(1024)S(1)} all-reduce(f32[2048]{0:T(1024)S(1)} %exponential_reduce_fusion.1), channel_id=1, replica_groups=mesh['row'=32,'col'=8] {'col'}, use_global_device_ids=true, to_apply=%region_15.0 | all-reduce | flops 2048 | bytes 16384 | tf_op jit(solution)/shard_map/psum | solution.py:25
  732.4 0.0 copy-start.1
  732.5 8.0 fusion.3
  740.5 78.0 %pmax.31 = f32[2048]{0:T(1024)S(1)} all-reduce(f32[2048]{0:T(1024)S(1)} %fusion.3), channel_id=1, replica_groups=mesh['row'=32,'col'=8] {'row'}, use_global_device_ids=true, to_apply=%region_17.0 | all-reduce | flops 2048 | bytes 16384 | tf_op jit(solution)/shard_map/pmax | solution.py:31
  818.5 8.2 exponential_reduce_fusion
  826.7 0.0 copy-done.1
  826.7 70.9 %psum.47 = f32[2048]{0:T(1024)S(1)} all-reduce(f32[2048]{0:T(1024)S(1)} %exponential_reduce_fusion), channel_id=1, replica_groups=mesh['row'=32,'col'=8] {'row'}, use_global_device_ids=true, to_apply=%region_19.0 | all-reduce | flops 2048 | bytes 16384 | tf_op jit(solution)/shard_map/psum | solution.py:32
  897.6 0.6 multiply_subtract_fusion
  (6 shorter events, 0.1 us)
Async XLA Ops:
  7.2 457.4 %copy-start.2 = (f32[2048]{0:T(1024)S(1)}, f32[2048]{0:T(1024)}, u32[]{:S(2)}) copy-start(f32[2048]{0:T(1024)} %param.7) | copy-start | bytes 24580
  7.2 42.9 %all-gather.4.cloned.1.call-start = ((), (), s32[]{:S(2)}) async-start(), calls=%async_computation | async-start | bytes 1179648 | tf_op jit(solution)/shard_map/all_gather | solution.py:37
  7.9 101.4 %all-gather.6.cloned.1.call-start = ((), (), s32[]{:S(2)}) async-start(), calls=%async_computation.3 | async-start | bytes 1081344 | tf_op jit(solution)/shard_map/all_gather | solution.py:38
  8.7 379.3 %all-reduce.3.cloned.1.call-start = ((), (), s32[]{:S(2)}) async-start(), calls=%async_computation.1 | async-start | bytes 2228224 | tf_op jit(solution)/shard_map/psum | solution.py:47
  50.1 409.9 %copy-start = (f32[128,2048]{1,0:T(8,128)S(1)}, f32[128,2048]{1,0:T(8,128)}, u32[]{:S(2)}) copy-start(f32[128,2048]{1,0:T(8,128)} %all-gather.4.cloned.1.call-done) | copy-start | bytes 3145732
  57.4 402.6 %all-reduce.5.cloned.1.call-start = ((), (), s32[]{:S(2)}) async-start(), calls=%async_computation.2 | async-start | bytes 278528 | tf_op jit(solution)/shard_map/psum | solution.py:51
  732.4 94.2 %copy-start.1 = (f32[2048]{0:T(1024)}, f32[2048]{0:T(1024)S(1)}, u32[]{:S(2)}) copy-start(f32[2048]{0:T(1024)S(1)} %multiply_subtract_fusion.1) | copy-start | bytes 24580
Sparse Core Ops, SparseCore 0:
  9.8 40.2 all-gather.3
  52.6 56.6 all-gather.5
  111.9 275.9 all-reduce.2
  390.7 69.2 all-reduce.4
where the time goes:
time: 905 us
  waiting for transfers between devices  441 us (49%)
  blocking collectives  358 us (40%)
  other arithmetic  59.1 us (7%)
  matrix products  31.3 us (3%)
  between operations  14 us (2%)
    psum x1, waiting for transfers between devices, local(): panel_sum = lax.psum(panel_sum, 'row')  277 us
    pmax x2, blocking collectives, across_sources(): highest = lax.pmax(highest, 'row')  162 us
    psum x2, blocking collectives, across_sources(): lax.psum(jnp.sum(jnp.exp(values - highest[None, :]), axis=0), 'row')  141 us
    psum x1, waiting for transfers between devices, local(): core_matrix = lax.psum(core_part, 'col')  69.3 us
    all_gather x1, waiting for transfers between devices, local(): tgt_full = lax.all_gather(tgt_pos, 'row', axis=0, tiled=True)  51.8 us
    all_gather x1, waiting for transfers between devices, local(): src_full = lax.all_gather(src_pos, 'col', axis=0, tiled=True)  41.4 us
    psum x2, blocking collectives, across_targets(): lax.psum(jnp.sum(jnp.exp(values - highest[:, None]), axis=1), 'col')  28.5 us
    pmax x2, blocking collectives, across_targets(): highest = lax.pmax(highest, 'col')  26 us
  transfers between devices with their start and end apart: 4, of which 4 were waited for; matrix products, arithmetic and copies ran while one was open for 1% of the time, Pallas kernels for 0%

commit v1 on v0

v1 whole, which is shorter than its diff:
```python
import math

import jax
import jax.numpy as jnp
from jax import lax
from jax.experimental import pallas as pl
from jax.experimental.pallas import tpu as pltpu
from jax.sharding import PartitionSpec as P

SWEEPS = 2
EPSILON = 0.25
LOG2E = 1.4426950408889634
MESH = pl.DeviceIdType.MESH
F32 = jnp.float32
BF16 = jnp.bfloat16
LOW = -3.0e38

SRC, TGT_Z, TGT_Y, TGT_C, SCATTER, MIDDLE, SPREAD, ROWS, PAIR, CHIPS, LOCAL_W, LOCAL_S, LOCAL_T = (
    0, 1, 2, 3, 4, 5, 6, 7, 9, 11, 13, 14, 15,
)


def split(value):
    high = value.astype(BF16)
    return high, (value - high.astype(F32)).astype(BF16)


def feature_major(x_ref, stack):
    size = x_ref.shape[1]

    def block(b, carry):
        cols = pl.ds(pl.multiple_of(b * 512, 512), 512)
        x = x_ref[:, cols]
        high, low = split(x)
        stack[0:128, cols] = high
        stack[128:256, cols] = low
        stack[256:384, cols] = high
        q = jnp.sum(x * x, axis=0, keepdims=True)
        q_high = q.astype(BF16).astype(F32)
        q_low = q - q_high
        at = lax.broadcasted_iota(jnp.int32, (16, 512), 0)
        ext = jnp.where((at == 1) | (at == 5), 1.0, 0.0)
        ext = jnp.where((at == 0) | (at == 4), q_high, ext)
        ext = jnp.where(at == 2, q_low, ext)
        stack[384:400, cols] = ext.astype(BF16)
        stack[400:512, cols] = jnp.zeros((112, 512), BF16)
        return carry

    lax.fori_loop(0, size // 512, block, 0)


def state_major(x_ref, stack):
    size = x_ref.shape[1]

    def block(b, carry):
        at = pl.ds(pl.multiple_of(b * 128, 128), 128)
        x = x_ref[:, at].T
        high, low = split(x)
        stack[at, 0:128] = high
        stack[at, 128:256] = low
        stack[at, 256:384] = high
        q = jnp.sum(x * x, axis=1, keepdims=True)
        q_high = q.astype(BF16).astype(F32)
        q_low = q - q_high
        lane = lax.broadcasted_iota(jnp.int32, (128, 128), 1)
        ext = jnp.where((lane == 1) | (lane == 5), 1.0, 0.0)
        ext = jnp.where((lane == 0) | (lane == 4), q_high, ext)
        ext = jnp.where(lane == 2, q_low, ext)
        stack[at, 384:512] = ext.astype(BF16)
        return carry

    lax.fori_loop(0, size // 128, block, 0)


def down_rows(vector, out):
    for b in range(vector.shape[0]):
        out[128 * b : 128 * (b + 1), :] = jnp.broadcast_to(vector[b : b + 1, :], (128, 128)).T


CHUNK = 64
STRIP = 256


def reduce_strip(n, pot, cost, out):
    lanes = pl.ds(pl.multiple_of(n * STRIP, STRIP), STRIP)

    def chunk(k, carry):
        top, summed = carry
        rows = pl.ds(pl.multiple_of(k * CHUNK, CHUNK), CHUNK)
        p = pot[rows, :]
        values = jnp.concatenate([p] * (STRIP // 128), axis=1) - cost[rows, lanes]
        values = values.reshape(CHUNK // 8, 8, STRIP)
        now = jnp.maximum(top, jnp.max(values, axis=0))
        summed = summed * jnp.exp2(top - now) + jnp.sum(jnp.exp2(values - now[None]), axis=0)
        return now, summed

    start = (jnp.full((8, STRIP), LOW, F32), jnp.zeros((8, STRIP), F32))
    top, summed = lax.fori_loop(0, cost.shape[0] // CHUNK, chunk, start, unroll=4)
    highest = jnp.max(top, axis=0, keepdims=True)
    total = jnp.sum(summed * jnp.exp2(top - highest), axis=0, keepdims=True)
    result = highest + LOG2E * jnp.log(total)
    for t in range(STRIP // 128):
        out[pl.ds(n * (STRIP // 128) + t, 1), :] = result[:, 128 * t : 128 * (t + 1)]


def combine(buffer):
    n = buffer.shape[0]
    top = buffer[0]
    for k in range(1, n):
        top = jnp.maximum(top, buffer[k])
    total = jnp.exp2(buffer[0] - top)
    for k in range(1, n):
        total = total + jnp.exp2(buffer[k] - top)
    return top + LOG2E * jnp.log(total)


def kernel(
    n_row, n_col, src_ref, tgt_ref, coupling_ref, prior_ref, f_ref, g_ref,
    weights, src_full, tgt_blocks, tgt_full, xs, xt, ys, yt, us, ut, panel,
    parts, gathered, middle, core, cost, cost_t, pot, local, by_col, by_pair, by_chip,
    send, recv,
):
    row, col = lax.axis_index("row"), lax.axis_index("col")
    core_id = lax.rem(row, 2)
    chip = row // 2
    n_chip = n_row // 2
    depth = lax.rem(chip, 4)
    y = chip // 4
    n_y = n_chip // 4
    sib = row + 1 - 2 * core_id
    rows_here, cols_here = coupling_ref.shape
    total_src, total_tgt = rows_here * n_row, cols_here * n_col
    group = 2 * n_col
    slot = core_id * n_col + col

    col_peers = [(row, lax.rem(col + d, n_col)) for d in range(1, n_col)]
    z_peers = [((y * 4 + lax.rem(depth + d, 4)) * 2 + core_id, col) for d in range(1, 4)]
    y_peers = [((lax.rem(y + d, n_y) * 4 + depth) * 2 + core_id, col) for d in range(1, n_y)]
    chip_peers = [(lax.rem(chip + d, n_chip) * 2 + core_id, col) for d in range(1, n_chip)]
    pair_peer = (sib, col)
    group_peers = col_peers + [(sib, lax.rem(col + d, n_col)) for d in range(n_col)]

    def put(source, target, index, peer):
        pltpu.make_async_remote_copy(
            src_ref=source, dst_ref=target, send_sem=send.at[index], recv_sem=recv.at[index],
            device_id=peer, device_id_type=MESH,
        ).start()

    def await_recv(ref, index):
        pltpu.make_async_copy(ref, ref, recv.at[index]).wait()

    def await_send(ref, index):
        pltpu.make_async_copy(ref, ref, send.at[index]).wait()

    barrier = pltpu.get_barrier_semaphore()
    greeted = group_peers + chip_peers
    for peer in greeted:
        pl.semaphore_signal(barrier, inc=1, device_id=peer, device_id_type=MESH)
    features = src_ref.shape[0]
    mine = pl.ds(pl.multiple_of(col * features, features), features)
    copy_w = pltpu.make_async_copy(coupling_ref, weights, recv.at[LOCAL_W])
    copy_s = pltpu.make_async_copy(src_ref, src_full.at[mine], recv.at[LOCAL_S])
    copy_t = pltpu.make_async_copy(tgt_ref, tgt_blocks.at[core_id, chip], recv.at[LOCAL_T])
    copy_t.start()
    copy_s.start()
    copy_w.start()
    pl.semaphore_wait(barrier, len(greeted))

    for peer in z_peers:
        put(tgt_ref, tgt_blocks.at[core_id, chip], TGT_Z, peer)
    for peer in col_peers:
        put(src_ref, src_full.at[mine], SRC, peer)
    copy_t.wait()
    await_recv(tgt_blocks.at[0, 0:3], TGT_Z)
    plane = pl.ds(y * 4, 4)
    for peer in y_peers:
        put(tgt_blocks.at[core_id, plane], tgt_blocks.at[core_id, plane], TGT_Y, peer)

    copy_s.wait()
    await_recv(src_full.at[0 : features * (n_col - 1)], SRC)
    await_recv(tgt_blocks.at[0, 0 : 4 * (n_y - 1)], TGT_Y)
    put(tgt_blocks.at[core_id], tgt_blocks.at[core_id], TGT_C, pair_peer)
    feature_major(src_full, xs)
    copy_w.wait()

    def panel_strip(n, carry):
        cols = pl.ds(pl.multiple_of(n * 256, 256), 256)
        panel[:, cols] = jnp.dot(xs[256:400, :], weights[:, cols], preferred_element_type=F32)
        return carry

    lax.fori_loop(0, cols_here // 256, panel_strip, 0)

    await_recv(tgt_blocks.at[0], TGT_C)
    for k in range(n_chip):
        tgt_full[8 * k : 8 * k + 8, :] = jnp.concatenate([tgt_blocks[0, k], tgt_blocks[1, k]], axis=0)
    feature_major(tgt_full, ys)

    part = jnp.zeros((144, 256), F32)
    whole = panel[...]
    for _ in range(3):
        term = whole.astype(BF16)
        whole = whole - term.astype(F32)
        part = part + lax.dot_general(
            term, ys[256:512, :], (((1,), (1,)), ((), ())), preferred_element_type=F32
        )
    at8 = lax.broadcasted_iota(jnp.int32, (8, 128), 0)
    lane8 = lax.broadcasted_iota(jnp.int32, (8, 128), 1)
    edge = jnp.where(at8 < 2, part[128:136, 0:128], 0.0)
    corner = part[128:136, 128:256]
    corner = jnp.concatenate([corner[6:8], corner[0:6]], axis=0)
    edge = jnp.where((at8 >= 2) & (at8 < 4), corner, edge)
    side = jnp.where(at8 < 2, part[0:128, 128:256].T[0:8], 0.0)
    for s in range(group):
        parts[s, 0:8, :] = part[8 * s : 8 * s + 8, 0:128]
        one = edge[s : s + 1] if s < 8 else side[s - 8 : s - 7]
        parts[s, 8:16, :] = jnp.where(at8 == 0, one, 0.0)

    def slot_of(peer):
        return lax.rem(peer[0], 2) * n_col + peer[1]

    for peer in group_peers:
        put(parts.at[slot_of(peer)], gathered.at[slot], SCATTER, peer)
    gathered[slot] = parts[slot]
    state_major(src_full, xt)
    await_recv(gathered.at[0 : group - 1], SCATTER)
    total = gathered[0]
    for k in range(1, group):
        total = total + gathered[k]
    middle[chip] = total
    for peer in chip_peers:
        put(middle.at[chip], middle.at[chip], MIDDLE, peer)
    state_major(tgt_full, yt)
    down_rows(prior_ref[...] * (LOG2E / EPSILON), pot)
    await_recv(middle.at[0 : n_chip - 1], MIDDLE)
    total = middle[0]
    for k in range(1, n_chip):
        total = total + middle[k]
    core[slot] = total
    for peer in group_peers:
        put(core.at[slot], core.at[slot], SPREAD, peer)
    await_recv(core.at[0 : group - 1], SPREAD)

    scale = -2.0 * LOG2E / (EPSILON * total_src * total_tgt)
    main = jnp.concatenate([core[s, 0:8, :] for s in range(group)], axis=0) * (4.0 * scale)
    src_q, src_one = core[0, 8:9, :], core[1, 8:9, :]
    corner_q, corner_one = core[2, 8:9, :], core[3, 8:9, :]
    tgt_q, tgt_one = core[8, 8:9, :], core[9, 8:9, :]

    def pattern(at, first, second):
        value = jnp.where((at == 0) | (at == 2) | (at == 4), first, 0.0)
        return jnp.where((at == 1) | (at == 5), second, value)

    at16 = lax.broadcasted_iota(jnp.int32, (128, 128), 0)
    lane16 = lax.broadcasted_iota(jnp.int32, (128, 128), 1)
    lower_left = pattern(at16, src_one, src_q) * (-2.0 * scale)
    upper_right = pattern(at16, tgt_one, tgt_q).T * (-2.0 * scale)
    lower_right = pattern(
        at16,
        pattern(lane16, corner_one[:, 1:2], corner_one[:, 0:1]),
        pattern(lane16, corner_q[:, 1:2], corner_q[:, 0:1]),
    ) * scale
    left = jnp.concatenate([main, lower_left], axis=0)
    right = jnp.concatenate([upper_right, lower_right], axis=0)
    left_high, left_low = split(left)
    right_high, right_low = split(right)
    right_lane = lax.broadcasted_iota(jnp.int32, (256, 128), 1)
    ext = jnp.where(right_lane < 4, right_high.astype(F32), right_low.astype(F32)).astype(BF16)
    factor = jnp.concatenate([left_high, left_high, left_low, ext], axis=1)

    def factor_t(b, carry):
        at = pl.ds(pl.multiple_of(b * 256, 256), 256)
        u = lax.dot_general(yt[at, :], factor, (((1,), (1,)), ((), ())), preferred_element_type=F32)
        high, low = split(u[:, 0:128])
        ut[at, 0:128] = high
        ut[at, 128:256] = high
        ut[at, 256:384] = low
        high, low = split(u[:, 128:256])
        lane = lax.broadcasted_iota(jnp.int32, (256, 128), 1)
        ut[at, 384:512] = jnp.where(lane < 4, high.astype(F32), low.astype(F32)).astype(BF16)
        return carry

    lax.fori_loop(0, cols_here // 256, factor_t, 0)

    def row_strip(n, carry):
        lanes = pl.ds(pl.multiple_of(n * STRIP, STRIP), STRIP)
        cost_t[:, lanes] = jnp.dot(ut[...], xs[:, lanes], preferred_element_type=F32)
        reduce_strip(n, pot, cost_t, local)
        return carry

    lax.fori_loop(0, rows_here // STRIP, row_strip, 0)

    def make_cost():
        def factor_n(b, carry):
            cols = pl.ds(pl.multiple_of(b * 256, 256), 256)
            u = jnp.dot(factor, ys[:, cols], preferred_element_type=F32)
            high, low = split(u[0:128])
            us[0:128, cols] = high
            us[128:256, cols] = high
            us[256:384, cols] = low
            high, low = split(u[128:256])
            at = lax.broadcasted_iota(jnp.int32, (128, 256), 0)
            us[384:512, cols] = jnp.where(at < 4, high.astype(F32), low.astype(F32)).astype(BF16)
            lanes = cols
            cost[:, lanes] = jnp.dot(xt[...], us[:, lanes], preferred_element_type=F32)
            return carry

        lax.fori_loop(0, cols_here // 256, factor_n, 0)

    def strip_pass(cost_ref):
        def body(n, carry):
            reduce_strip(n, pot, cost_ref, local)
            return carry

        lax.fori_loop(0, cost_ref.shape[1] // STRIP, body, 0)

    for sweep in range(SWEEPS):
        if sweep:
            strip_pass(cost_t)
        by_col[sweep, col] = local[...]
        for peer in col_peers:
            put(by_col.at[sweep, col], by_col.at[sweep, col], ROWS + sweep, peer)
        if sweep == 0:
            make_cost()
        await_recv(by_col.at[sweep, 0 : n_col - 1], ROWS + sweep)
        f = -math.log2(total_src) - combine(by_col.at[sweep])
        down_rows(f, pot)
        strip_pass(cost)
        by_pair[sweep, core_id] = local[...]
        put(by_pair.at[sweep, core_id], by_pair.at[sweep, core_id], PAIR + sweep, pair_peer)
        await_recv(by_pair.at[sweep, 0], PAIR + sweep)
        by_chip[sweep, chip] = combine(by_pair.at[sweep])
        for peer in chip_peers:
            put(by_chip.at[sweep, chip], by_chip.at[sweep, chip], CHIPS + sweep, peer)
        await_recv(by_chip.at[sweep, 0 : n_chip - 1], CHIPS + sweep)
        g = -math.log2(total_tgt) - combine(by_chip.at[sweep])
        if sweep + 1 < SWEEPS:
            down_rows(g, pot)
    f_ref[...] = f * (EPSILON / LOG2E)
    g_ref[...] = g * (EPSILON / LOG2E)

    await_send(src_full.at[0 : features * (n_col - 1)], SRC)
    await_send(tgt_blocks.at[0, 0:3], TGT_Z)
    await_send(tgt_blocks.at[0, 0 : 4 * (n_y - 1)], TGT_Y)
    await_send(tgt_blocks.at[0], TGT_C)
    await_send(gathered.at[0 : group - 1], SCATTER)
    await_send(middle.at[0 : n_chip - 1], MIDDLE)
    await_send(core.at[0 : group - 1], SPREAD)
    for sweep in range(SWEEPS):
        await_send(by_col.at[sweep, 0 : n_col - 1], ROWS + sweep)
        await_send(by_pair.at[sweep, 0], PAIR + sweep)
        await_send(by_chip.at[sweep, 0 : n_chip - 1], CHIPS + sweep)


def solution(mesh):
    n_row, n_col = mesh.shape["row"], mesh.shape["col"]
    n_chip = n_row // 2
    group = 2 * n_col

    def local(src_pos, tgt_pos, coupling, prior_tgt):
        rows, cols = coupling.shape
        vmem = pl.BlockSpec(memory_space=pltpu.VMEM)
        anywhere = pl.BlockSpec(memory_space=pl.ANY)
        f, g = pl.pallas_call(
            lambda *refs: kernel(n_row, n_col, *refs),
            out_shape=[
                jax.ShapeDtypeStruct((rows // 128, 128), F32),
                jax.ShapeDtypeStruct((cols // 128, 128), F32),
            ],
            in_specs=[anywhere, anywhere, anywhere, vmem],
            out_specs=[vmem, vmem],
            scratch_shapes=[
                pltpu.VMEM((rows, cols), BF16),
                pltpu.VMEM((128, rows), F32),
                pltpu.VMEM((2, n_chip, 4, cols), F32),
                pltpu.VMEM((128, cols), F32),
                pltpu.VMEM((512, rows), BF16),
                pltpu.VMEM((rows, 512), BF16),
                pltpu.VMEM((512, cols), BF16),
                pltpu.VMEM((cols, 512), BF16),
                pltpu.VMEM((512, cols), BF16),
                pltpu.VMEM((cols, 512), BF16),
                pltpu.VMEM((144, cols), F32),
                pltpu.VMEM((group, 16, 128), F32),
                pltpu.VMEM((group, 16, 128), F32),
                pltpu.VMEM((n_chip, 16, 128), F32),
                pltpu.VMEM((group, 16, 128), F32),
                pltpu.VMEM((rows, cols), F32),
                pltpu.VMEM((cols, rows), F32),
                pltpu.VMEM((max(rows, cols), 128), F32),
                pltpu.VMEM((max(rows, cols) // 128, 128), F32),
                pltpu.VMEM((SWEEPS, n_col, rows // 128, 128), F32),
                pltpu.VMEM((SWEEPS, 2, cols // 128, 128), F32),
                pltpu.VMEM((SWEEPS, n_chip, cols // 128, 128), F32),
                pltpu.SemaphoreType.DMA((16,)),
                pltpu.SemaphoreType.DMA((16,)),
            ],
            compiler_params=pltpu.CompilerParams(
                collective_id=0, has_side_effects=True, vmem_limit_bytes=63 * 2**20
            ),
        )(src_pos, tgt_pos, coupling, prior_tgt.reshape(cols // 128, 128))
        return f.reshape(rows), g.reshape(cols)

    placed = (P("col", "row"), P("row", "col"), P("row", "col"), P("col"))
    return jax.shard_map(
        local, mesh=mesh, in_specs=placed, out_specs=(P("row"), P("col")), check_vma=False
    )
```

time: 905 us -> 109 us (0.12)
  waiting for transfers between devices: 441 us -> 0 us
  blocking collectives: 358 us -> 0 us
  Pallas kernels: 0 us -> 105 us
  other arithmetic: 59.1 us -> 0 us
  matrix products: 31.3 us -> 0 us
  between operations: 14 us -> 0.64 us
    psum x2 -> x0, waiting for transfers between devices: 346 us -> none  [the longest x1 277 us: local(): panel_sum = lax.psum(panel_sum, 'row')]
    pmax x4 -> x0, blocking collectives: 188 us -> none  [the longest x2 162 us: across_sources(): highest = lax.pmax(highest, 'row')]
    psum x4 -> x0, blocking collectives: 170 us -> none  [the longest x2 141 us: across_sources(): lax.psum(jnp.sum(jnp.exp(values - highest[None, :]), axis=0), 'row')]
    pallas_call x0 -> x1, Pallas kernels: none -> 105 us  [local(): pl.pallas_call(lambda *refs: kernel(n_row, n_col, *refs), out_shape=[jax....]
    all_gather x2 -> x0, waiting for transfers between devices: 93.2 us -> none  [the longest x1 51.8 us: local(): tgt_full = lax.all_gather(tgt_pos, 'row', axis=0, tiled=True)]
    reduce_sum x4 -> x0, other arithmetic: 32.8 us -> none  [the longest x2 16.4 us: across_targets(): jnp.sum(jnp.exp(values - highest[:, None]), axis=1)]
    dot_general x4 -> x0, matrix products: 31.3 us -> none  [the longest x1 18.2 us: local(): jnp.dot(rows_core, tgt_left, precision=lax.Precision.HIGHEST)]
    reduce_max x3 -> x0, other arithmetic: 24 us -> none  [the longest x2 16 us: across_sources(): highest = jnp.max(values, axis=0)]
  transfers between devices with their start and end apart: 4 -> 0, of which waited for: 4 -> 0; matrix products, arithmetic and copies ran while one was open for 1% -> 0% of each run, Pallas kernels for 0% -> 0%
where the time goes in v1:
time: 109 us; the launch traced here: 108 us
  Pallas kernels  105 us (96%)
  local copies, waits for them, and re-layouts  2.59 us (2%)
    pallas_call x1, Pallas kernels, local(): pl.pallas_call(lambda *refs: kernel(n_row, n_col, *refs), out_shape=[jax....  105 us
    unnamed x2, local copies, waits for them, and re-layouts  2.59 us

profile of v1, /device:TPU:1, one launch (start us, length us, event | category | flops | bytes accessed | tf_op | source)
XLA Modules:
  0.0 108.5 jit_solution(14611959693059092473)
XLA Ops:
  0.6 105.3 %shard_map.59 = (f32[16,128]{1,0:T(8,128)}, f32[16,128]{1,0:T(8,128)}) custom-call(f32[16,2048]{1,0:T(8,128)} %refs_0_.1, f32[4,2048]{1,0:T(4,128)} %refs_1_.1, bf16[2048,2048]{1,0:T(8,128)(2,1)} %refs_2_.1, f32[16,128]{1,0:T(8,128)} %bitcast.3), custom_call_target="tpu_custom_call" | custom-call | tf_op jit(solution)/shard_map/pallas_call | solution.py:363
  105.9 1.3 %copy.8 = f32[2048]{0:T(1024)} copy(f32[2048]{0:T(1024)} %bitcast.5) | data formatting | bytes 16384
  107.2 1.3 %copy.9 = f32[2048]{0:T(1024)} copy(f32[2048]{0:T(1024)} %bitcast.4) | data formatting | bytes 16384

commit v2 on v1

--- a/solution.py
+++ b/solution.py
@@ -18,6 +18,7 @@
 SRC, TGT_Z, TGT_Y, TGT_C, SCATTER, MIDDLE, SPREAD, ROWS, PAIR, CHIPS, LOCAL_W, LOCAL_S, LOCAL_T = (
     0, 1, 2, 3, 4, 5, 6, 7, 9, 11, 13, 14, 15,
 )
+SRC_Z, TGT_Z2, TGT_Y2 = 16, 17, 18
 
 
 def split(value):
@@ -133,9 +134,15 @@
     group = 2 * n_col
     slot = core_id * n_col + col
 
+    x_size = n_col // 2
+    x_at, plane_half = lax.rem(col, x_size), col // x_size
+    half_col = (1 - plane_half) * x_size + x_at
+    x_peers = [(row, plane_half * x_size + lax.rem(x_at + d, x_size)) for d in range(1, x_size)]
+    half_peer = (row, half_col)
+    z_near = [((y * 4 + lax.rem(depth + d, 4)) * 2 + core_id, col) for d in (1, 3)]
+    z_far = ((y * 4 + lax.rem(depth + 2, 4)) * 2 + core_id, col)
+    y_peers = [((lax.rem(y + d, n_y) * 4 + depth) * 2 + core_id, col) for d in range(1, n_y)]
     col_peers = [(row, lax.rem(col + d, n_col)) for d in range(1, n_col)]
-    z_peers = [((y * 4 + lax.rem(depth + d, 4)) * 2 + core_id, col) for d in range(1, 4)]
-    y_peers = [((lax.rem(y + d, n_y) * 4 + depth) * 2 + core_id, col) for d in range(1, n_y)]
     chip_peers = [(lax.rem(chip + d, n_chip) * 2 + core_id, col) for d in range(1, n_chip)]
     pair_peer = (sib, col)
     group_peers = col_peers + [(sib, lax.rem(col + d, n_col)) for d in range(n_col)]
@@ -153,11 +160,12 @@
         pltpu.make_async_copy(ref, ref, send.at[index]).wait()
 
     barrier = pltpu.get_barrier_semaphore()
-    greeted = group_peers + chip_peers
+    greeted = x_peers + y_peers + z_near + [half_peer, pair_peer]
     for peer in greeted:
         pl.semaphore_signal(barrier, inc=1, device_id=peer, device_id_type=MESH)
     features = src_ref.shape[0]
     mine = pl.ds(pl.multiple_of(col * features, features), features)
+    halfs = pl.ds(pl.multiple_of(half_col * features, features), features)
     copy_w = pltpu.make_async_copy(coupling_ref, weights, recv.at[LOCAL_W])
     copy_s = pltpu.make_async_copy(src_ref, src_full.at[mine], recv.at[LOCAL_S])
     copy_t = pltpu.make_async_copy(tgt_ref, tgt_blocks.at[core_id, chip], recv.at[LOCAL_T])
@@ -166,19 +174,30 @@
     copy_w.start()
     pl.semaphore_wait(barrier, len(greeted))
 
-    for peer in z_peers:
+    for peer in z_near:
         put(tgt_ref, tgt_blocks.at[core_id, chip], TGT_Z, peer)
-    for peer in col_peers:
+    put(src_ref, src_full.at[mine], SRC_Z, half_peer)
+    for peer in x_peers:
         put(src_ref, src_full.at[mine], SRC, peer)
     copy_t.wait()
-    await_recv(tgt_blocks.at[0, 0:3], TGT_Z)
-    plane = pl.ds(y * 4, 4)
+    await_recv(tgt_blocks.at[0, 0:2], TGT_Z)
+    put(tgt_ref, tgt_blocks.at[core_id, chip], TGT_Z2, z_far)
+    for d in (0, 1, 3):
+        at = y * 4 + lax.rem(depth + d, 4)
+        for peer in y_peers:
+            put(tgt_blocks.at[core_id, at], tgt_blocks.at[core_id, at], TGT_Y, peer)
+    await_recv(src_full.at[0:features], SRC_Z)
+    for peer in x_peers:
+        put(src_full.at[halfs], src_full.at[halfs], SRC, peer)
+    await_recv(tgt_blocks.at[0, 0], TGT_Z2)
+    at = y * 4 + lax.rem(depth + 2, 4)
     for peer in y_peers:
-        put(tgt_blocks.at[core_id, plane], tgt_blocks.at[core_id, plane], TGT_Y, peer)
+        put(tgt_blocks.at[core_id, at], tgt_blocks.at[core_id, at], TGT_Y2, peer)
 
     copy_s.wait()
-    await_recv(src_full.at[0 : features * (n_col - 1)], SRC)
-    await_recv(tgt_blocks.at[0, 0 : 4 * (n_y - 1)], TGT_Y)
+    await_recv(src_full.at[0 : features * (n_col - 2)], SRC)
+    await_recv(tgt_blocks.at[0, 0 : 3 * (n_y - 1)], TGT_Y)
+    await_recv(tgt_blocks.at[0, 0 : n_y - 1], TGT_Y2)
     put(tgt_blocks.at[core_id], tgt_blocks.at[core_id], TGT_C, pair_peer)
     feature_major(src_full, xs)
     copy_w.wait()
@@ -338,9 +357,12 @@
     f_ref[...] = f * (EPSILON / LOG2E)
     g_ref[...] = g * (EPSILON / LOG2E)
 
-    await_send(src_full.at[0 : features * (n_col - 1)], SRC)
-    await_send(tgt_blocks.at[0, 0:3], TGT_Z)
-    await_send(tgt_blocks.at[0, 0 : 4 * (n_y - 1)], TGT_Y)
+    await_send(src_full.at[0:features], SRC_Z)
+    await_send(src_full.at[0 : features * (n_col - 2)], SRC)
+    await_send(tgt_blocks.at[0, 0:2], TGT_Z)
+    await_send(tgt_blocks.at[0, 0], TGT_Z2)
+    await_send(tgt_blocks.at[0, 0 : 3 * (n_y - 1)], TGT_Y)
+    await_send(tgt_blocks.at[0, 0 : n_y - 1], TGT_Y2)
     await_send(tgt_blocks.at[0], TGT_C)
     await_send(gathered.at[0 : group - 1], SCATTER)
     await_send(middle.at[0 : n_chip - 1], MIDDLE)
@@ -391,8 +413,8 @@
                 pltpu.VMEM((SWEEPS, n_col, rows // 128, 128), F32),
                 pltpu.VMEM((SWEEPS, 2, cols // 128, 128), F32),
                 pltpu.VMEM((SWEEPS, n_chip, cols // 128, 128), F32),
-                pltpu.SemaphoreType.DMA((16,)),
-                pltpu.SemaphoreType.DMA((16,)),
+                pltpu.SemaphoreType.DMA((19,)),
+                pltpu.SemaphoreType.DMA((19,)),
             ],
             compiler_params=pltpu.CompilerParams(
                 collective_id=0, has_side_effects=True, vmem_limit_bytes=63 * 2**20

time: 109 us -> 101 us (0.927)
  Pallas kernels: 105 us -> 97.9 us
    pallas_call x1, Pallas kernels: 105 us -> 97.9 us  [local(): pl.pallas_call(lambda *refs: kernel(n_row, n_col, *refs), out_shape=[jax....]
where the time goes in v2:
time: 101 us
  Pallas kernels  97.9 us (97%)
  local copies, waits for them, and re-layouts  2.59 us (3%)
    pallas_call x1, Pallas kernels, local(): pl.pallas_call(lambda *refs: kernel(n_row, n_col, *refs), out_shape=[jax....  97.9 us
    unnamed x2, local copies, waits for them, and re-layouts  2.59 us

profile of v2, /device:TPU:1, one launch (start us, length us, event | category | flops | bytes accessed | tf_op | source)
XLA Modules:
  0.0 101.1 jit_solution(14538913655678361659)
XLA Ops:
  0.6 97.9 %shard_map.59 = (f32[16,128]{1,0:T(8,128)}, f32[16,128]{1,0:T(8,128)}) custom-call(f32[16,2048]{1,0:T(8,128)} %refs_0_.1, f32[4,2048]{1,0:T(4,128)} %refs_1_.1, bf16[2048,2048]{1,0:T(8,128)(2,1)} %refs_2_.1, f32[16,128]{1,0:T(8,128)} %bitcast.3), custom_call_target="tpu_custom_call" | custom-call | tf_op jit(solution)/shard_map/pallas_call | solution.py:385
  98.5 1.3 %copy.8 = f32[2048]{0:T(1024)} copy(f32[2048]{0:T(1024)} %bitcast.5) | data formatting | bytes 16384
  99.8 1.3 %copy.9 = f32[2048]{0:T(1024)} copy(f32[2048]{0:T(1024)} %bitcast.4) | data formatting | bytes 16384

commit v3 on v2

--- a/solution.py
+++ b/solution.py
@@ -15,10 +15,9 @@
 BF16 = jnp.bfloat16
 LOW = -3.0e38
 
-SRC, TGT_Z, TGT_Y, TGT_C, SCATTER, MIDDLE, SPREAD, ROWS, PAIR, CHIPS, LOCAL_W, LOCAL_S, LOCAL_T = (
-    0, 1, 2, 3, 4, 5, 6, 7, 9, 11, 13, 14, 15,
-)
-SRC_Z, TGT_Z2, TGT_Y2 = 16, 17, 18
+TGT_Z, TGT_Z2, TGT_Y, TGT_Y2, TGT_C, SCATTER, MIDDLE, SPREAD, LOCAL_W, LOCAL_S, LOCAL_T = range(11)
+SRC, SRC_Z, ROWS, PAIR, CHIPS = 11, 13, 15, 19, 21
+SLOTS = 23
 
 
 def split(value):
@@ -26,9 +25,27 @@
     return high, (value - high.astype(F32)).astype(BF16)
 
 
+def extension(x, shape, axis):
+    q = jnp.sum(x * x, axis=axis, keepdims=True)
+    q_high = q.astype(BF16).astype(F32)
+    at = lax.broadcasted_iota(jnp.int32, shape, axis)
+    ext = jnp.where((at == 1) | (at == 5), 1.0, 0.0)
+    ext = jnp.where((at == 0) | (at == 4), q_high, ext)
+    return jnp.where(at == 2, q - q_high, ext).astype(BF16)
+
+
+def source_right(x_ref, stack, first, size):
+    def block(b, carry):
+        cols = pl.ds(pl.multiple_of(first + b * 512, 512), 512)
+        x = x_ref[:, cols]
+        stack[0:128, cols] = x.astype(BF16)
+        stack[128:144, cols] = extension(x, (16, 512), 0)
+        return carry
+
+    lax.fori_loop(0, size // 512, block, 0)
+
+
 def feature_major(x_ref, stack):
-    size = x_ref.shape[1]
-
     def block(b, carry):
         cols = pl.ds(pl.multiple_of(b * 512, 512), 512)
         x = x_ref[:, cols]
@@ -36,18 +53,11 @@
         stack[0:128, cols] = high
         stack[128:256, cols] = low
         stack[256:384, cols] = high
-        q = jnp.sum(x * x, axis=0, keepdims=True)
-        q_high = q.astype(BF16).astype(F32)
-        q_low = q - q_high
-        at = lax.broadcasted_iota(jnp.int32, (16, 512), 0)
-        ext = jnp.where((at == 1) | (at == 5), 1.0, 0.0)
-        ext = jnp.where((at == 0) | (at == 4), q_high, ext)
-        ext = jnp.where(at == 2, q_low, ext)
-        stack[384:400, cols] = ext.astype(BF16)
+        stack[384:400, cols] = extension(x, (16, 512), 0)
         stack[400:512, cols] = jnp.zeros((112, 512), BF16)
         return carry
 
-    lax.fori_loop(0, size // 512, block, 0)
+    lax.fori_loop(0, x_ref.shape[1] // 512, block, 0)
 
 
 def state_major(x_ref, stack):
@@ -60,34 +70,50 @@
         stack[at, 0:128] = high
         stack[at, 128:256] = low
         stack[at, 256:384] = high
-        q = jnp.sum(x * x, axis=1, keepdims=True)
-        q_high = q.astype(BF16).astype(F32)
-        q_low = q - q_high
-        lane = lax.broadcasted_iota(jnp.int32, (128, 128), 1)
-        ext = jnp.where((lane == 1) | (lane == 5), 1.0, 0.0)
-        ext = jnp.where((lane == 0) | (lane == 4), q_high, ext)
-        ext = jnp.where(lane == 2, q_low, ext)
-        stack[at, 384:512] = ext.astype(BF16)
+        stack[at, 384:512] = extension(x, (128, 128), 1)
         return carry
 
     lax.fori_loop(0, size // 128, block, 0)
 
 
-def down_rows(vector, out):
+def down_rows(vector, out, first):
     for b in range(vector.shape[0]):
-        out[128 * b : 128 * (b + 1), :] = jnp.broadcast_to(vector[b : b + 1, :], (128, 128)).T
-
-
-CHUNK = 64
+        at = first + 128 * b
+        out[at : at + 128, :] = jnp.broadcast_to(vector[b : b + 1, :], (128, 128)).T
+
+
+def tree(op, terms):
+    while len(terms) > 1:
+        terms = [op(*terms[k : k + 2]) if k + 1 < len(terms) else terms[k] for k in range(0, len(terms), 2)]
+    return terms[0]
+
+
+def row_block(at, pot, cost):
+    n = cost.shape[1] // 128
+    pieces = []
+    for q in range(16):
+        rows = pl.ds(pl.multiple_of(at + 8 * q, 8), 8)
+        values = [pot[t : t + 1, :] - cost[rows, 128 * t : 128 * (t + 1)] for t in range(n)]
+        top = tree(jnp.maximum, values)
+        summed = tree(jnp.add, [jnp.exp2(v - top) for v in values])
+        highest = jnp.max(top, axis=1, keepdims=True)
+        total = jnp.sum(summed * jnp.exp2(top - highest), axis=1, keepdims=True)
+        pieces.append(highest + LOG2E * jnp.log(total))
+    column = jnp.concatenate(pieces, axis=0)
+    eye = lax.broadcasted_iota(jnp.int32, (128, 128), 0) == lax.broadcasted_iota(jnp.int32, (128, 128), 1)
+    return jnp.sum(jnp.where(eye, column, 0.0), axis=0, keepdims=True)
+
+
+CHUNK = 128
 STRIP = 256
 
 
-def reduce_strip(n, pot, cost, out):
+def col_strip(n, first, size, pot, cost, tops, sums, out):
     lanes = pl.ds(pl.multiple_of(n * STRIP, STRIP), STRIP)
 
     def chunk(k, carry):
         top, summed = carry
-        rows = pl.ds(pl.multiple_of(k * CHUNK, CHUNK), CHUNK)
+        rows = pl.ds(pl.multiple_of(first + k * CHUNK, CHUNK), CHUNK)
         p = pot[rows, :]
         values = jnp.concatenate([p] * (STRIP // 128), axis=1) - cost[rows, lanes]
         values = values.reshape(CHUNK // 8, 8, STRIP)
@@ -95,8 +121,15 @@
         summed = summed * jnp.exp2(top - now) + jnp.sum(jnp.exp2(values - now[None]), axis=0)
         return now, summed
 
-    start = (jnp.full((8, STRIP), LOW, F32), jnp.zeros((8, STRIP), F32))
-    top, summed = lax.fori_loop(0, cost.shape[0] // CHUNK, chunk, start, unroll=4)
+    if first == 0:
+        start = (jnp.full((8, STRIP), LOW, F32), jnp.zeros((8, STRIP), F32))
+    else:
+        start = (tops[:, lanes], sums[:, lanes])
+    top, summed = lax.fori_loop(0, size // CHUNK, chunk, start, unroll=4)
+    if out is None:
+        tops[:, lanes] = top
+        sums[:, lanes] = summed
+        return
     highest = jnp.max(top, axis=0, keepdims=True)
     total = jnp.sum(summed * jnp.exp2(top - highest), axis=0, keepdims=True)
     result = highest + LOG2E * jnp.log(total)
@@ -117,8 +150,8 @@
 
 def kernel(
     n_row, n_col, src_ref, tgt_ref, coupling_ref, prior_ref, f_ref, g_ref,
-    weights, src_full, tgt_blocks, tgt_full, xs, xt, ys, yt, us, ut, panel,
-    parts, gathered, middle, core, cost, cost_t, pot, local, by_col, by_pair, by_chip,
+    weights, src_full, tgt_blocks, tgt_full, xs, xt, ys, us, panel,
+    parts, gathered, middle, core, cost, pot, pot_tgt, tops, sums, by_col, by_pair, by_chip,
     send, recv,
 ):
     row, col = lax.axis_index("row"), lax.axis_index("col")
@@ -176,9 +209,12 @@
 
     for peer in z_near:
         put(tgt_ref, tgt_blocks.at[core_id, chip], TGT_Z, peer)
-    put(src_ref, src_full.at[mine], SRC_Z, half_peer)
-    for peer in x_peers:
-        put(src_ref, src_full.at[mine], SRC, peer)
+    half = rows_here // 2
+    halves = [slice(0, half), slice(half, rows_here)]
+    for h, cols in enumerate(halves):
+        put(src_ref.at[:, cols], src_full.at[mine, cols], SRC_Z + h, half_peer)
+        for peer in x_peers:
+            put(src_ref.at[:, cols], src_full.at[mine, cols], SRC + h, peer)
     copy_t.wait()
     await_recv(tgt_blocks.at[0, 0:2], TGT_Z)
     put(tgt_ref, tgt_blocks.at[core_id, chip], TGT_Z2, z_far)
@@ -186,29 +222,36 @@
         at = y * 4 + lax.rem(depth + d, 4)
         for peer in y_peers:
             put(tgt_blocks.at[core_id, at], tgt_blocks.at[core_id, at], TGT_Y, peer)
-    await_recv(src_full.at[0:features], SRC_Z)
-    for peer in x_peers:
-        put(src_full.at[halfs], src_full.at[halfs], SRC, peer)
+    for h, cols in enumerate(halves):
+        await_recv(src_full.at[0:features, cols], SRC_Z + h)
+        for peer in x_peers:
+            put(src_full.at[halfs, cols], src_full.at[halfs, cols], SRC + h, peer)
     await_recv(tgt_blocks.at[0, 0], TGT_Z2)
     at = y * 4 + lax.rem(depth + 2, 4)
     for peer in y_peers:
         put(tgt_blocks.at[core_id, at], tgt_blocks.at[core_id, at], TGT_Y2, peer)
 
     copy_s.wait()
-    await_recv(src_full.at[0 : features * (n_col - 2)], SRC)
+    copy_w.wait()
+
+    def panel_part(cols, more):
+        def panel_strip(n, carry):
+            at = pl.ds(pl.multiple_of(n * 256, 256), 256)
+            term = jnp.dot(xs[:, cols], weights[cols, at], preferred_element_type=F32)
+            panel[:, at] = panel[:, at] + term if more else term
+            return carry
+
+        lax.fori_loop(0, cols_here // 256, panel_strip, 0)
+
+    await_recv(src_full.at[0 : features * (n_col - 2), halves[0]], SRC)
+    source_right(src_full, xs, 0, half)
+    panel_part(halves[0], False)
     await_recv(tgt_blocks.at[0, 0 : 3 * (n_y - 1)], TGT_Y)
     await_recv(tgt_blocks.at[0, 0 : n_y - 1], TGT_Y2)
     put(tgt_blocks.at[core_id], tgt_blocks.at[core_id], TGT_C, pair_peer)
-    feature_major(src_full, xs)
-    copy_w.wait()
-
-    def panel_strip(n, carry):
-        cols = pl.ds(pl.multiple_of(n * 256, 256), 256)
-        panel[:, cols] = jnp.dot(xs[256:400, :], weights[:, cols], preferred_element_type=F32)
-        return carry
-
-    lax.fori_loop(0, cols_here // 256, panel_strip, 0)
-
+    await_recv(src_full.at[0 : features * (n_col - 2), halves[1]], SRC + 1)
+    source_right(src_full, xs, half, half)
+    panel_part(halves[1], True)
     await_recv(tgt_blocks.at[0], TGT_C)
     for k in range(n_chip):
         tgt_full[8 * k : 8 * k + 8, :] = jnp.concatenate([tgt_blocks[0, k], tgt_blocks[1, k]], axis=0)
@@ -248,8 +291,7 @@
     middle[chip] = total
     for peer in chip_peers:
         put(middle.at[chip], middle.at[chip], MIDDLE, peer)
-    state_major(tgt_full, yt)
-    down_rows(prior_ref[...] * (LOG2E / EPSILON), pot)
+    pot_tgt[...] = prior_ref[...] * (LOG2E / EPSILON)
     await_recv(middle.at[0 : n_chip - 1], MIDDLE)
     total = middle[0]
     for k in range(1, n_chip):
@@ -286,65 +328,55 @@
     ext = jnp.where(right_lane < 4, right_high.astype(F32), right_low.astype(F32)).astype(BF16)
     factor = jnp.concatenate([left_high, left_high, left_low, ext], axis=1)
 
-    def factor_t(b, carry):
-        at = pl.ds(pl.multiple_of(b * 256, 256), 256)
-        u = lax.dot_general(yt[at, :], factor, (((1,), (1,)), ((), ())), preferred_element_type=F32)
-        high, low = split(u[:, 0:128])
-        ut[at, 0:128] = high
-        ut[at, 128:256] = high
-        ut[at, 256:384] = low
-        high, low = split(u[:, 128:256])
-        lane = lax.broadcasted_iota(jnp.int32, (256, 128), 1)
-        ut[at, 384:512] = jnp.where(lane < 4, high.astype(F32), low.astype(F32)).astype(BF16)
+    def factor_strip(n):
+        cols = pl.ds(pl.multiple_of(n * 256, 256), 256)
+        u = jnp.dot(factor, ys[:, cols], preferred_element_type=F32)
+        high, low = split(u[0:128])
+        us[0:128, cols] = high
+        us[128:256, cols] = high
+        us[256:384, cols] = low
+        high, low = split(u[128:256])
+        at = lax.broadcasted_iota(jnp.int32, (128, 256), 0)
+        us[384:512, cols] = jnp.where(at < 4, high.astype(F32), low.astype(F32)).astype(BF16)
+
+    n_strips = cols_here // 256
+
+    def cost_strip(n, carry):
+        lanes = pl.ds(pl.multiple_of(n * 256, 256), 256)
+        cost[:, lanes] = jnp.dot(xt[...], us[:, lanes], preferred_element_type=F32)
         return carry
 
-    lax.fori_loop(0, cols_here // 256, factor_t, 0)
-
-    def row_strip(n, carry):
-        lanes = pl.ds(pl.multiple_of(n * STRIP, STRIP), STRIP)
-        cost_t[:, lanes] = jnp.dot(ut[...], xs[:, lanes], preferred_element_type=F32)
-        reduce_strip(n, pot, cost_t, local)
+    def factor_loop(n, carry):
+        factor_strip(n)
         return carry
 
-    lax.fori_loop(0, rows_here // STRIP, row_strip, 0)
-
-    def make_cost():
-        def factor_n(b, carry):
-            cols = pl.ds(pl.multiple_of(b * 256, 256), 256)
-            u = jnp.dot(factor, ys[:, cols], preferred_element_type=F32)
-            high, low = split(u[0:128])
-            us[0:128, cols] = high
-            us[128:256, cols] = high
-            us[256:384, cols] = low
-            high, low = split(u[128:256])
-            at = lax.broadcasted_iota(jnp.int32, (128, 256), 0)
-            us[384:512, cols] = jnp.where(at < 4, high.astype(F32), low.astype(F32)).astype(BF16)
-            lanes = cols
-            cost[:, lanes] = jnp.dot(xt[...], us[:, lanes], preferred_element_type=F32)
-            return carry
-
-        lax.fori_loop(0, cols_here // 256, factor_n, 0)
-
-    def strip_pass(cost_ref):
-        def body(n, carry):
-            reduce_strip(n, pot, cost_ref, local)
-            return carry
-
-        lax.fori_loop(0, cost_ref.shape[1] // STRIP, body, 0)
-
+    lax.fori_loop(0, n_strips, factor_loop, 0)
+    lax.fori_loop(0, n_strips, cost_strip, 0)
+
+    n_part = half // 128
     for sweep in range(SWEEPS):
-        if sweep:
-            strip_pass(cost_t)
-        by_col[sweep, col] = local[...]
-        for peer in col_peers:
-            put(by_col.at[sweep, col], by_col.at[sweep, col], ROWS + sweep, peer)
-        if sweep == 0:
-            make_cost()
-        await_recv(by_col.at[sweep, 0 : n_col - 1], ROWS + sweep)
-        f = -math.log2(total_src) - combine(by_col.at[sweep])
-        down_rows(f, pot)
-        strip_pass(cost)
-        by_pair[sweep, core_id] = local[...]
+        for h in range(2):
+            mine_now = by_col.at[sweep, h, col]
+
+            def block(b, carry):
+                mine_now[pl.ds(b, 1), :] = row_block(h * half + b * 128, pot_tgt, cost)
+                return carry
+
+            lax.fori_loop(0, n_part, block, 0)
+            for peer in col_peers:
+                put(mine_now, mine_now, ROWS + 2 * sweep + h, peer)
+        f = []
+        for h in range(2):
+            await_recv(by_col.at[sweep, h, 0 : n_col - 1], ROWS + 2 * sweep + h)
+            f.append(-math.log2(total_src) - combine(by_col.at[sweep, h]))
+            down_rows(f[h], pot, h * half)
+            out = by_pair.at[sweep, core_id] if h else None
+
+            def strip(n, carry):
+                col_strip(n, h * half, half, pot, cost, tops, sums, out)
+                return carry
+
+            lax.fori_loop(0, cols_here // STRIP, strip, 0)
         put(by_pair.at[sweep, core_id], by_pair.at[sweep, core_id], PAIR + sweep, pair_peer)
         await_recv(by_pair.at[sweep, 0], PAIR + sweep)
         by_chip[sweep, chip] = combine(by_pair.at[sweep])
@@ -352,13 +384,13 @@
             put(by_chip.at[sweep, chip], by_chip.at[sweep, chip], CHIPS + sweep, peer)
         await_recv(by_chip.at[sweep, 0 : n_chip - 1], CHIPS + sweep)
         g = -math.log2(total_tgt) - combine(by_chip.at[sweep])
-        if sweep + 1 < SWEEPS:
-            down_rows(g, pot)
-    f_ref[...] = f * (EPSILON / LOG2E)
+        pot_tgt[...] = g
+    f_ref[...] = jnp.concatenate(f, axis=0) * (EPSILON / LOG2E)
     g_ref[...] = g * (EPSILON / LOG2E)
 
-    await_send(src_full.at[0:features], SRC_Z)
-    await_send(src_full.at[0 : features * (n_col - 2)], SRC)
+    for h, cols in enumerate(halves):
+        await_send(src_full.at[0:features, cols], SRC_Z + h)
+        await_send(src_full.at[0 : features * (n_col - 2), cols], SRC + h)
     await_send(tgt_blocks.at[0, 0:2], TGT_Z)
     await_send(tgt_blocks.at[0, 0], TGT_Z2)
     await_send(tgt_blocks.at[0, 0 : 3 * (n_y - 1)], TGT_Y)
@@ -368,7 +400,8 @@
     await_send(middle.at[0 : n_chip - 1], MIDDLE)
     await_send(core.at[0 : group - 1], SPREAD)
     for sweep in range(SWEEPS):
-        await_send(by_col.at[sweep, 0 : n_col - 1], ROWS + sweep)
+        for h in range(2):
+            await_send(by_col.at[sweep, h, 0 : n_col - 1], ROWS + 2 * sweep + h)
         await_send(by_pair.at[sweep, 0], PAIR + sweep)
         await_send(by_chip.at[sweep, 0 : n_chip - 1], CHIPS + sweep)
 
@@ -395,26 +428,25 @@
                 pltpu.VMEM((128, rows), F32),
                 pltpu.VMEM((2, n_chip, 4, cols), F32),
                 pltpu.VMEM((128, cols), F32),
-                pltpu.VMEM((512, rows), BF16),
+                pltpu.VMEM((144, rows), BF16),
                 pltpu.VMEM((rows, 512), BF16),
                 pltpu.VMEM((512, cols), BF16),
-                pltpu.VMEM((cols, 512), BF16),
                 pltpu.VMEM((512, cols), BF16),
-                pltpu.VMEM((cols, 512), BF16),
                 pltpu.VMEM((144, cols), F32),
                 pltpu.VMEM((group, 16, 128), F32),
                 pltpu.VMEM((group, 16, 128), F32),
                 pltpu.VMEM((n_chip, 16, 128), F32),
                 pltpu.VMEM((group, 16, 128), F32),
                 pltpu.VMEM((rows, cols), F32),
-                pltpu.VMEM((cols, rows), F32),
-                pltpu.VMEM((max(rows, cols), 128), F32),
-                pltpu.VMEM((max(rows, cols) // 128, 128), F32),
-                pltpu.VMEM((SWEEPS, n_col, rows // 128, 128), F32),
+                pltpu.VMEM((rows, 128), F32),
+                pltpu.VMEM((cols // 128, 128), F32),
+                pltpu.VMEM((8, cols), F32),
+                pltpu.VMEM((8, cols), F32),
+                pltpu.VMEM((SWEEPS, 2, n_col, rows // 256, 128), F32),
                 pltpu.VMEM((SWEEPS, 2, cols // 128, 128), F32),
                 pltpu.VMEM((SWEEPS, n_chip, cols // 128, 128), F32),
-                pltpu.SemaphoreType.DMA((19,)),
-                pltpu.SemaphoreType.DMA((19,)),
+                pltpu.SemaphoreType.DMA((SLOTS,)),
+                pltpu.SemaphoreType.DMA((SLOTS,)),
             ],
             compiler_params=pltpu.CompilerParams(
                 collective_id=0, has_side_effects=True, vmem_limit_bytes=63 * 2**20

time: 101 us -> 96.2 us (0.952)
  Pallas kernels: 97.9 us -> 92.7 us
    pallas_call x1, Pallas kernels: 97.9 us -> 92.7 us  [local(): pl.pallas_call(lambda *refs: kernel(n_row, n_col, *refs), out_shape=[jax....]
where the time goes in v3:
time: 96.2 us; the launch traced here: 95.9 us
  Pallas kernels  92.7 us (96%)
  local copies, waits for them, and re-layouts  2.59 us (3%)
    pallas_call x1, Pallas kernels, local(): pl.pallas_call(lambda *refs: kernel(n_row, n_col, *refs), out_shape=[jax....  92.7 us
    unnamed x2, local copies, waits for them, and re-layouts  2.59 us

profile of v3, /device:TPU:1, one launch (start us, length us, event | category | flops | bytes accessed | tf_op | source)
XLA Modules:
  0.0 95.9 jit_solution(3477439014797511815)
XLA Ops:
  0.6 92.7 %shard_map.59 = (f32[16,128]{1,0:T(8,128)}, f32[16,128]{1,0:T(8,128)}) custom-call(f32[16,2048]{1,0:T(8,128)} %refs_0_.1, f32[4,2048]{1,0:T(4,128)} %refs_1_.1, bf16[2048,2048]{1,0:T(8,128)(2,1)} %refs_2_.1, f32[16,128]{1,0:T(8,128)} %bitcast.3), custom_call_target="tpu_custom_call" | custom-call | tf_op jit(solution)/shard_map/pallas_call | solution.py:418
  93.3 1.3 %copy.8 = f32[2048]{0:T(1024)} copy(f32[2048]{0:T(1024)} %bitcast.5) | data formatting | bytes 16384
  94.6 1.3 %copy.9 = f32[2048]{0:T(1024)} copy(f32[2048]{0:T(1024)} %bitcast.4) | data formatting | bytes 16384

commit v4 on v3

--- a/solution.py
+++ b/solution.py
@@ -16,8 +16,8 @@
 LOW = -3.0e38
 
 TGT_Z, TGT_Z2, TGT_Y, TGT_Y2, TGT_C, SCATTER, MIDDLE, SPREAD, LOCAL_W, LOCAL_S, LOCAL_T = range(11)
-SRC, SRC_Z, ROWS, PAIR, CHIPS = 11, 13, 15, 19, 21
-SLOTS = 23
+SRC_Z, ROWS, PAIR, CHIPS, NEAR, FAR = 11, 13, 17, 19, 21, 29
+SLOTS = 33
 
 
 def split(value):
@@ -88,20 +88,19 @@
     return terms[0]
 
 
-def row_block(at, pot, cost):
-    n = cost.shape[1] // 128
-    pieces = []
-    for q in range(16):
-        rows = pl.ds(pl.multiple_of(at + 8 * q, 8), 8)
-        values = [pot[t : t + 1, :] - cost[rows, 128 * t : 128 * (t + 1)] for t in range(n)]
-        top = tree(jnp.maximum, values)
-        summed = tree(jnp.add, [jnp.exp2(v - top) for v in values])
-        highest = jnp.max(top, axis=1, keepdims=True)
-        total = jnp.sum(summed * jnp.exp2(top - highest), axis=1, keepdims=True)
-        pieces.append(highest + LOG2E * jnp.log(total))
-    column = jnp.concatenate(pieces, axis=0)
-    eye = lax.broadcasted_iota(jnp.int32, (128, 128), 0) == lax.broadcasted_iota(jnp.int32, (128, 128), 1)
-    return jnp.sum(jnp.where(eye, column, 0.0), axis=0, keepdims=True)
+def row_partial(at, pot, cost, tops, sums):
+    rows = pl.ds(pl.multiple_of(at, 8), 8)
+    values = [pot[t : t + 1, :] - cost[rows, 128 * t : 128 * (t + 1)] for t in range(cost.shape[1] // 128)]
+    top = tree(jnp.maximum, values)
+    tops[rows, :] = top
+    sums[rows, :] = tree(jnp.add, [jnp.exp2(v - top) for v in values])
+
+
+def row_finish(at, tops, sums):
+    top = tops[at : at + 128, :].T
+    highest = jnp.max(top, axis=0, keepdims=True)
+    total = jnp.sum(sums[at : at + 128, :].T * jnp.exp2(top - highest), axis=0, keepdims=True)
+    return highest + LOG2E * jnp.log(total)
 
 
 CHUNK = 128
@@ -151,7 +150,7 @@
 def kernel(
     n_row, n_col, src_ref, tgt_ref, coupling_ref, prior_ref, f_ref, g_ref,
     weights, src_full, tgt_blocks, tgt_full, xs, xt, ys, us, panel,
-    parts, gathered, middle, core, cost, pot, pot_tgt, tops, sums, by_col, by_pair, by_chip,
+    parts, gathered, middle, core, cost, pot, pot_tgt, tops, sums, row_tops, row_sums, by_col, by_pair, by_chip,
     send, recv,
 ):
     row, col = lax.axis_index("row"), lax.axis_index("col")
@@ -170,7 +169,8 @@
     x_size = n_col // 2
     x_at, plane_half = lax.rem(col, x_size), col // x_size
     half_col = (1 - plane_half) * x_size + x_at
-    x_peers = [(row, plane_half * x_size + lax.rem(x_at + d, x_size)) for d in range(1, x_size)]
+    next_x, last_x = lax.rem(x_at + 1, x_size), lax.rem(x_at + x_size - 1, x_size)
+    x_near = [(row, plane_half * x_size + next_x), (row, plane_half * x_size + last_x)]
     half_peer = (row, half_col)
     z_near = [((y * 4 + lax.rem(depth + d, 4)) * 2 + core_id, col) for d in (1, 3)]
     z_far = ((y * 4 + lax.rem(depth + 2, 4)) * 2 + core_id, col)
@@ -193,12 +193,11 @@
         pltpu.make_async_copy(ref, ref, send.at[index]).wait()
 
     barrier = pltpu.get_barrier_semaphore()
-    greeted = x_peers + y_peers + z_near + [half_peer, pair_peer]
+    greeted = x_near + y_peers + z_near + [half_peer, pair_peer]
     for peer in greeted:
         pl.semaphore_signal(barrier, inc=1, device_id=peer, device_id_type=MESH)
     features = src_ref.shape[0]
     mine = pl.ds(pl.multiple_of(col * features, features), features)
-    halfs = pl.ds(pl.multiple_of(half_col * features, features), features)
     copy_w = pltpu.make_async_copy(coupling_ref, weights, recv.at[LOCAL_W])
     copy_s = pltpu.make_async_copy(src_ref, src_full.at[mine], recv.at[LOCAL_S])
     copy_t = pltpu.make_async_copy(tgt_ref, tgt_blocks.at[core_id, chip], recv.at[LOCAL_T])
@@ -211,25 +210,57 @@
         put(tgt_ref, tgt_blocks.at[core_id, chip], TGT_Z, peer)
     half = rows_here // 2
     halves = [slice(0, half), slice(half, rows_here)]
-    for h, cols in enumerate(halves):
-        put(src_ref.at[:, cols], src_full.at[mine, cols], SRC_Z + h, half_peer)
-        for peer in x_peers:
-            put(src_ref.at[:, cols], src_full.at[mine, cols], SRC + h, peer)
+    def block_at(c, h):
+        return src_full.at[pl.ds(pl.multiple_of(c * features, features), features), halves[h]]
+
+    def near(c, h, k, source=None):
+        for d in range(2):
+            put(source or block_at(c, h), block_at(c, h), NEAR + 4 * (1 - d) + 2 * k + h, x_near[d])
+
+    def onward(h, k):
+        d = 1 - h
+        side = plane_half if k == 0 else 1 - plane_half
+        block = block_at(side * x_size + (last_x if d else next_x), h)
+        await_recv(block, NEAR + 4 * d + 2 * k + h)
+        put(block, block, FAR + 2 * k + h, x_near[1 - d])
+
+    def arrived(h):
+        for k in range(2):
+            await_recv(block_at(col, h), NEAR + 4 * h + 2 * k + h)
+            await_recv(block_at(col, h), FAR + 2 * k + h)
+
+    def plane_block(d):
+        return tgt_blocks.at[core_id, y * 4 + lax.rem(depth + d, 4)]
+
+    for h in range(2):
+        own = src_ref.at[:, halves[h]]
+        put(own, block_at(col, h), SRC_Z + h, half_peer)
+        near(col, h, 0, own)
     copy_t.wait()
     await_recv(tgt_blocks.at[0, 0:2], TGT_Z)
     put(tgt_ref, tgt_blocks.at[core_id, chip], TGT_Z2, z_far)
     for d in (0, 1, 3):
-        at = y * 4 + lax.rem(depth + d, 4)
         for peer in y_peers:
-            put(tgt_blocks.at[core_id, at], tgt_blocks.at[core_id, at], TGT_Y, peer)
-    for h, cols in enumerate(halves):
-        await_recv(src_full.at[0:features, cols], SRC_Z + h)
-        for peer in x_peers:
-            put(src_full.at[halfs, cols], src_full.at[halfs, cols], SRC + h, peer)
+            put(plane_block(d), plane_block(d), TGT_Y, peer)
+    await_recv(block_at(col, 0), SRC_Z)
+    near(half_col, 0, 1)
+    onward(0, 0)
+    await_recv(block_at(col, 1), SRC_Z + 1)
+    near(half_col, 1, 1)
+    onward(1, 0)
+    for d in (0, 1, 3):
+        put(plane_block(d), plane_block(d), TGT_C, pair_peer)
     await_recv(tgt_blocks.at[0, 0], TGT_Z2)
-    at = y * 4 + lax.rem(depth + 2, 4)
     for peer in y_peers:
-        put(tgt_blocks.at[core_id, at], tgt_blocks.at[core_id, at], TGT_Y2, peer)
+        put(plane_block(2), plane_block(2), TGT_Y2, peer)
+    put(plane_block(2), plane_block(2), TGT_C, pair_peer)
+    onward(0, 1)
+    onward(1, 1)
+    await_recv(tgt_blocks.at[0, 0 : 3 * (n_y - 1)], TGT_Y)
+    for e in range(1, n_y):
+        for d in (0, 1, 3):
+            block = tgt_blocks.at[core_id, lax.rem(y + e, n_y) * 4 + lax.rem(depth + d, 4)]
+            put(block, block, TGT_C, pair_peer)
 
     copy_s.wait()
     copy_w.wait()
@@ -243,13 +274,14 @@
 
         lax.fori_loop(0, cols_here // 256, panel_strip, 0)
 
-    await_recv(src_full.at[0 : features * (n_col - 2), halves[0]], SRC)
+    arrived(0)
     source_right(src_full, xs, 0, half)
     panel_part(halves[0], False)
-    await_recv(tgt_blocks.at[0, 0 : 3 * (n_y - 1)], TGT_Y)
     await_recv(tgt_blocks.at[0, 0 : n_y - 1], TGT_Y2)
-    put(tgt_blocks.at[core_id], tgt_blocks.at[core_id], TGT_C, pair_peer)
-    await_recv(src_full.at[0 : features * (n_col - 2), halves[1]], SRC + 1)
+    for e in range(1, n_y):
+        block = tgt_blocks.at[core_id, lax.rem(y + e, n_y) * 4 + lax.rem(depth + 2, 4)]
+        put(block, block, TGT_C, pair_peer)
+    arrived(1)
     source_right(src_full, xs, half, half)
     panel_part(halves[1], True)
     await_recv(tgt_blocks.at[0], TGT_C)
@@ -359,10 +391,13 @@
             mine_now = by_col.at[sweep, h, col]
 
             def block(b, carry):
-                mine_now[pl.ds(b, 1), :] = row_block(h * half + b * 128, pot_tgt, cost)
+                for q in range(8):
+                    row_partial(h * half + b * 64 + 8 * q, pot_tgt, cost, row_tops, row_sums)
                 return carry
 
-            lax.fori_loop(0, n_part, block, 0)
+            lax.fori_loop(0, half // 64, block, 0)
+            for b in range(n_part):
+                mine_now[b : b + 1, :] = row_finish(h * half + 128 * b, row_tops, row_sums)
             for peer in col_peers:
                 put(mine_now, mine_now, ROWS + 2 * sweep + h, peer)
         f = []
@@ -388,9 +423,12 @@
     f_ref[...] = jnp.concatenate(f, axis=0) * (EPSILON / LOG2E)
     g_ref[...] = g * (EPSILON / LOG2E)
 
-    for h, cols in enumerate(halves):
-        await_send(src_full.at[0:features, cols], SRC_Z + h)
-        await_send(src_full.at[0 : features * (n_col - 2), cols], SRC + h)
+    for h in range(2):
+        await_send(block_at(col, h), SRC_Z + h)
+        for k in range(2):
+            await_send(block_at(col, h), FAR + 2 * k + h)
+            for d in range(2):
+                await_send(block_at(col, h), NEAR + 4 * d + 2 * k + h)
     await_send(tgt_blocks.at[0, 0:2], TGT_Z)
     await_send(tgt_blocks.at[0, 0], TGT_Z2)
     await_send(tgt_blocks.at[0, 0 : 3 * (n_y - 1)], TGT_Y)
@@ -442,6 +480,8 @@
                 pltpu.VMEM((cols // 128, 128), F32),
                 pltpu.VMEM((8, cols), F32),
                 pltpu.VMEM((8, cols), F32),
+                pltpu.VMEM((rows, 128), F32),
+                pltpu.VMEM((rows, 128), F32),
                 pltpu.VMEM((SWEEPS, 2, n_col, rows // 256, 128), F32),
                 pltpu.VMEM((SWEEPS, 2, cols // 128, 128), F32),
                 pltpu.VMEM((SWEEPS, n_chip, cols // 128, 128), F32),

time: 96.2 us -> 93.9 us (0.976)
  Pallas kernels: 92.7 us -> 90.5 us
    pallas_call x1, Pallas kernels: 92.7 us -> 90.5 us  [local(): pl.pallas_call(lambda *refs: kernel(n_row, n_col, *refs), out_shape=[jax....]
where the time goes in v4:
time: 93.9 us; the launch traced here: 93.7 us
  Pallas kernels  90.5 us (96%)
  local copies, waits for them, and re-layouts  2.59 us (3%)
    pallas_call x1, Pallas kernels, local(): pl.pallas_call(lambda *refs: kernel(n_row, n_col, *refs), out_shape=[jax....  90.5 us
    unnamed x2, local copies, waits for them, and re-layouts  2.59 us

profile of v4, /device:TPU:1, one launch (start us, length us, event | category | flops | bytes accessed | tf_op | source)
XLA Modules:
  0.0 93.7 jit_solution(11355173632198719487)
XLA Ops:
  0.6 90.5 %shard_map.59 = (f32[16,128]{1,0:T(8,128)}, f32[16,128]{1,0:T(8,128)}) custom-call(f32[16,2048]{1,0:T(8,128)} %refs_0_.1, f32[4,2048]{1,0:T(4,128)} %refs_1_.1, bf16[2048,2048]{1,0:T(8,128)(2,1)} %refs_2_.1, f32[16,128]{1,0:T(8,128)} %bitcast.3), custom_call_target="tpu_custom_call" | custom-call | tf_op jit(solution)/shard_map/pallas_call | solution.py:456
  91.1 1.3 %copy.8 = f32[2048]{0:T(1024)} copy(f32[2048]{0:T(1024)} %bitcast.5) | data formatting | bytes 16384
  92.4 1.3 %copy.9 = f32[2048]{0:T(1024)} copy(f32[2048]{0:T(1024)} %bitcast.4) | data formatting | bytes 16384

commit v5 on v4

--- a/solution.py
+++ b/solution.py
@@ -149,7 +149,7 @@
 
 def kernel(
     n_row, n_col, src_ref, tgt_ref, coupling_ref, prior_ref, f_ref, g_ref,
-    weights, src_full, tgt_blocks, tgt_full, xs, xt, ys, us, panel,
+    weights, src_full, tgt_blocks, tgt_full, xs, xt, ys, us, terms,
     parts, gathered, middle, core, cost, pot, pot_tgt, tops, sums, row_tops, row_sums, by_col, by_pair, by_chip,
     send, recv,
 ):
@@ -173,7 +173,6 @@
     x_near = [(row, plane_half * x_size + next_x), (row, plane_half * x_size + last_x)]
     half_peer = (row, half_col)
     z_near = [((y * 4 + lax.rem(depth + d, 4)) * 2 + core_id, col) for d in (1, 3)]
-    z_far = ((y * 4 + lax.rem(depth + 2, 4)) * 2 + core_id, col)
     y_peers = [((lax.rem(y + d, n_y) * 4 + depth) * 2 + core_id, col) for d in range(1, n_y)]
     col_peers = [(row, lax.rem(col + d, n_col)) for d in range(1, n_col)]
     chip_peers = [(lax.rem(chip + d, n_chip) * 2 + core_id, col) for d in range(1, n_chip)]
@@ -200,14 +199,15 @@
     mine = pl.ds(pl.multiple_of(col * features, features), features)
     copy_w = pltpu.make_async_copy(coupling_ref, weights, recv.at[LOCAL_W])
     copy_s = pltpu.make_async_copy(src_ref, src_full.at[mine], recv.at[LOCAL_S])
-    copy_t = pltpu.make_async_copy(tgt_ref, tgt_blocks.at[core_id, chip], recv.at[LOCAL_T])
+    copy_t = pltpu.make_async_copy(tgt_ref, tgt_blocks.at[core_id, y, 0], recv.at[LOCAL_T])
     copy_t.start()
     copy_s.start()
     copy_w.start()
     pl.semaphore_wait(barrier, len(greeted))
 
-    for peer in z_near:
-        put(tgt_ref, tgt_blocks.at[core_id, chip], TGT_Z, peer)
+    plane = tgt_blocks.at[core_id, y]
+    for d in range(2):
+        put(tgt_ref, plane.at[2 - d], TGT_Z, z_near[d])
     half = rows_here // 2
     halves = [slice(0, half), slice(half, rows_here)]
     def block_at(c, h):
@@ -229,74 +229,54 @@
             await_recv(block_at(col, h), NEAR + 4 * h + 2 * k + h)
             await_recv(block_at(col, h), FAR + 2 * k + h)
 
-    def plane_block(d):
-        return tgt_blocks.at[core_id, y * 4 + lax.rem(depth + d, 4)]
-
     for h in range(2):
         own = src_ref.at[:, halves[h]]
         put(own, block_at(col, h), SRC_Z + h, half_peer)
         near(col, h, 0, own)
     copy_t.wait()
-    await_recv(tgt_blocks.at[0, 0:2], TGT_Z)
-    put(tgt_ref, tgt_blocks.at[core_id, chip], TGT_Z2, z_far)
-    for d in (0, 1, 3):
-        for peer in y_peers:
-            put(plane_block(d), plane_block(d), TGT_Y, peer)
+    await_recv(tgt_blocks.at[0, 0, 0:2], TGT_Z)
+    put(plane.at[2], plane.at[3], TGT_Z2, z_near[0])
+    for peer in y_peers:
+        put(plane.at[0:3], plane.at[0:3], TGT_Y, peer)
     await_recv(block_at(col, 0), SRC_Z)
     near(half_col, 0, 1)
     onward(0, 0)
     await_recv(block_at(col, 1), SRC_Z + 1)
     near(half_col, 1, 1)
     onward(1, 0)
-    for d in (0, 1, 3):
-        put(plane_block(d), plane_block(d), TGT_C, pair_peer)
-    await_recv(tgt_blocks.at[0, 0], TGT_Z2)
+    await_recv(tgt_blocks.at[0, 0, 0], TGT_Z2)
     for peer in y_peers:
-        put(plane_block(2), plane_block(2), TGT_Y2, peer)
-    put(plane_block(2), plane_block(2), TGT_C, pair_peer)
+        put(plane.at[3], plane.at[3], TGT_Y2, peer)
     onward(0, 1)
     onward(1, 1)
-    await_recv(tgt_blocks.at[0, 0 : 3 * (n_y - 1)], TGT_Y)
+    put(plane, plane, TGT_C, pair_peer)
+    await_recv(tgt_blocks.at[0, 0 : n_y - 1, 0:3], TGT_Y)
     for e in range(1, n_y):
-        for d in (0, 1, 3):
-            block = tgt_blocks.at[core_id, lax.rem(y + e, n_y) * 4 + lax.rem(depth + d, 4)]
-            put(block, block, TGT_C, pair_peer)
-
+        block = tgt_blocks.at[core_id, lax.rem(y + e, n_y), 0:3]
+        put(block, block, TGT_C, pair_peer)
+    await_recv(tgt_blocks.at[0, 0 : n_y - 1, 3], TGT_Y2)
+    for e in range(1, n_y):
+        block = tgt_blocks.at[core_id, lax.rem(y + e, n_y), 3]
+        put(block, block, TGT_C, pair_peer)
+    arrived(0)
+    arrived(1)
     copy_s.wait()
     copy_w.wait()
 
-    def panel_part(cols, more):
-        def panel_strip(n, carry):
-            at = pl.ds(pl.multiple_of(n * 256, 256), 256)
-            term = jnp.dot(xs[:, cols], weights[cols, at], preferred_element_type=F32)
-            panel[:, at] = panel[:, at] + term if more else term
-            return carry
-
-        lax.fori_loop(0, cols_here // 256, panel_strip, 0)
-
-    arrived(0)
-    source_right(src_full, xs, 0, half)
-    panel_part(halves[0], False)
-    await_recv(tgt_blocks.at[0, 0 : n_y - 1], TGT_Y2)
-    for e in range(1, n_y):
-        block = tgt_blocks.at[core_id, lax.rem(y + e, n_y) * 4 + lax.rem(depth + 2, 4)]
-        put(block, block, TGT_C, pair_peer)
-    arrived(1)
-    source_right(src_full, xs, half, half)
-    panel_part(halves[1], True)
+    source_right(src_full, xs, 0, rows_here)
     await_recv(tgt_blocks.at[0], TGT_C)
     for k in range(n_chip):
-        tgt_full[8 * k : 8 * k + 8, :] = jnp.concatenate([tgt_blocks[0, k], tgt_blocks[1, k]], axis=0)
+        away = lax.rem(k % 4 - depth + 4, 4)
+        at = away + (away // 2) * (5 - 2 * away)
+        tgt_full[8 * k : 8 * k + 8, :] = jnp.concatenate([tgt_blocks[0, k // 4, at], tgt_blocks[1, k // 4, at]], axis=0)
     feature_major(tgt_full, ys)
 
-    part = jnp.zeros((144, 256), F32)
-    whole = panel[...]
-    for _ in range(3):
-        term = whole.astype(BF16)
-        whole = whole - term.astype(F32)
-        part = part + lax.dot_general(
-            term, ys[256:512, :], (((1,), (1,)), ((), ())), preferred_element_type=F32
-        )
+    mixed = lax.dot_general(
+        weights[...], ys[256:512, :], (((1,), (1,)), ((), ())), preferred_element_type=F32
+    )
+    terms[:, 0:256], terms[:, 256:512] = split(mixed)
+    part = jnp.dot(xs[...], terms[...], preferred_element_type=F32)
+    part = part[:, 0:256] + part[:, 256:512]
     at8 = lax.broadcasted_iota(jnp.int32, (8, 128), 0)
     lane8 = lax.broadcasted_iota(jnp.int32, (8, 128), 1)
     edge = jnp.where(at8 < 2, part[128:136, 0:128], 0.0)
@@ -429,10 +409,10 @@
             await_send(block_at(col, h), FAR + 2 * k + h)
             for d in range(2):
                 await_send(block_at(col, h), NEAR + 4 * d + 2 * k + h)
-    await_send(tgt_blocks.at[0, 0:2], TGT_Z)
-    await_send(tgt_blocks.at[0, 0], TGT_Z2)
-    await_send(tgt_blocks.at[0, 0 : 3 * (n_y - 1)], TGT_Y)
-    await_send(tgt_blocks.at[0, 0 : n_y - 1], TGT_Y2)
+    await_send(tgt_blocks.at[0, 0, 0:2], TGT_Z)
+    await_send(tgt_blocks.at[0, 0, 0], TGT_Z2)
+    await_send(tgt_blocks.at[0, 0 : n_y - 1, 0:3], TGT_Y)
+    await_send(tgt_blocks.at[0, 0 : n_y - 1, 3], TGT_Y2)
     await_send(tgt_blocks.at[0], TGT_C)
     await_send(gathered.at[0 : group - 1], SCATTER)
     await_send(middle.at[0 : n_chip - 1], MIDDLE)
@@ -464,13 +444,13 @@
             scratch_shapes=[
                 pltpu.VMEM((rows, cols), BF16),
                 pltpu.VMEM((128, rows), F32),
-                pltpu.VMEM((2, n_chip, 4, cols), F32),
+                pltpu.VMEM((2, n_chip // 4, 4, 4, cols), F32),
                 pltpu.VMEM((128, cols), F32),
                 pltpu.VMEM((144, rows), BF16),
                 pltpu.VMEM((rows, 512), BF16),
                 pltpu.VMEM((512, cols), BF16),
                 pltpu.VMEM((512, cols), BF16),
-                pltpu.VMEM((144, cols), F32),
+                pltpu.VMEM((rows, 512), BF16),
                 pltpu.VMEM((group, 16, 128), F32),
                 pltpu.VMEM((group, 16, 128), F32),
                 pltpu.VMEM((n_chip, 16, 128), F32),

time: 93.9 us -> 92.1 us (0.981)
  Pallas kernels: 90.5 us -> 88.6 us
    pallas_call x1, Pallas kernels: 90.5 us -> 88.6 us  [local(): pl.pallas_call(lambda *refs: kernel(n_row, n_col, *refs), out_shape=[jax....]
where the time goes in v5:
time: 92.1 us; the launch traced here: 91.8 us
  Pallas kernels  88.6 us (96%)
  local copies, waits for them, and re-layouts  2.59 us (3%)
    pallas_call x1, Pallas kernels, local(): pl.pallas_call(lambda *refs: kernel(n_row, n_col, *refs), out_shape=[jax....  88.6 us
    unnamed x2, local copies, waits for them, and re-layouts  2.59 us

profile of v5, /device:TPU:1, one launch (start us, length us, event | category | flops | bytes accessed | tf_op | source)
XLA Modules:
  0.0 91.8 jit_solution(8770489334150174535)
XLA Ops:
  0.6 88.6 %shard_map.59 = (f32[16,128]{1,0:T(8,128)}, f32[16,128]{1,0:T(8,128)}) custom-call(f32[16,2048]{1,0:T(8,128)} %refs_0_.1, f32[4,2048]{1,0:T(4,128)} %refs_1_.1, bf16[2048,2048]{1,0:T(8,128)(2,1)} %refs_2_.1, f32[16,128]{1,0:T(8,128)} %bitcast.3), custom_call_target="tpu_custom_call" | custom-call | tf_op jit(solution)/shard_map/pallas_call | solution.py:436
  89.3 1.3 %copy.8 = f32[2048]{0:T(1024)} copy(f32[2048]{0:T(1024)} %bitcast.5) | data formatting | bytes 16384
  90.6 1.3 %copy.9 = f32[2048]{0:T(1024)} copy(f32[2048]{0:T(1024)} %bitcast.4) | data formatting | bytes 16384

commit v6 on v5

--- a/solution.py
+++ b/solution.py
@@ -16,8 +16,8 @@
 LOW = -3.0e38
 
 TGT_Z, TGT_Z2, TGT_Y, TGT_Y2, TGT_C, SCATTER, MIDDLE, SPREAD, LOCAL_W, LOCAL_S, LOCAL_T = range(11)
-SRC_Z, ROWS, PAIR, CHIPS, NEAR, FAR = 11, 13, 17, 19, 21, 29
-SLOTS = 33
+SRC_Z, ROWS, PAIR, CHIPS, NEAR, FAR = 11, 13, 17, 21, 25, 33
+SLOTS = 37
 
 
 def split(value):
@@ -107,8 +107,8 @@
 STRIP = 256
 
 
-def col_strip(n, first, size, pot, cost, tops, sums, out):
-    lanes = pl.ds(pl.multiple_of(n * STRIP, STRIP), STRIP)
+def col_strip(n, lane, first, size, pot, cost, tops, sums, out):
+    lanes = pl.ds(pl.multiple_of(lane + n * STRIP, STRIP), STRIP)
 
     def chunk(k, carry):
         top, summed = carry
@@ -353,19 +353,21 @@
 
     n_strips = cols_here // 256
 
-    def cost_strip(n, carry):
+    def cost_of(n):
         lanes = pl.ds(pl.multiple_of(n * 256, 256), 256)
         cost[:, lanes] = jnp.dot(xt[...], us[:, lanes], preferred_element_type=F32)
+
+    def cost_strip(n, carry):
+        cost_of(n)
+        factor_strip(n + 1)
         return carry
 
-    def factor_loop(n, carry):
-        factor_strip(n)
-        return carry
-
-    lax.fori_loop(0, n_strips, factor_loop, 0)
-    lax.fori_loop(0, n_strips, cost_strip, 0)
+    factor_strip(0)
+    lax.fori_loop(0, n_strips - 1, cost_strip, 0)
+    cost_of(n_strips - 1)
 
     n_part = half // 128
+    n_lanes = cols_here // 2
     for sweep in range(SWEEPS):
         for h in range(2):
             mine_now = by_col.at[sweep, h, col]
@@ -385,23 +387,30 @@
             await_recv(by_col.at[sweep, h, 0 : n_col - 1], ROWS + 2 * sweep + h)
             f.append(-math.log2(total_src) - combine(by_col.at[sweep, h]))
             down_rows(f[h], pot, h * half)
-            out = by_pair.at[sweep, core_id] if h else None
-
-            def strip(n, carry):
-                col_strip(n, h * half, half, pot, cost, tops, sums, out)
-                return carry
-
-            lax.fori_loop(0, cols_here // STRIP, strip, 0)
-        put(by_pair.at[sweep, core_id], by_pair.at[sweep, core_id], PAIR + sweep, pair_peer)
-        await_recv(by_pair.at[sweep, 0], PAIR + sweep)
-        by_chip[sweep, chip] = combine(by_pair.at[sweep])
-        for peer in chip_peers:
-            put(by_chip.at[sweep, chip], by_chip.at[sweep, chip], CHIPS + sweep, peer)
-        await_recv(by_chip.at[sweep, 0 : n_chip - 1], CHIPS + sweep)
-        g = -math.log2(total_tgt) - combine(by_chip.at[sweep])
-        pot_tgt[...] = g
+
+            for j in range(2):
+                out = by_pair.at[sweep, j, core_id] if h else None
+
+                def strip(n, carry):
+                    col_strip(n, j * n_lanes, h * half, half, pot, cost, tops, sums, out)
+                    return carry
+
+                lax.fori_loop(0, n_lanes // STRIP, strip, 0)
+                if h:
+                    put(out, out, PAIR + 2 * sweep + j, pair_peer)
+        for j in range(2):
+            await_recv(by_pair.at[sweep, j, 0], PAIR + 2 * sweep + j)
+            mine_now = by_chip.at[sweep, j, chip]
+            mine_now[...] = combine(by_pair.at[sweep, j])
+            for peer in chip_peers:
+                put(mine_now, mine_now, CHIPS + 2 * sweep + j, peer)
+        g = []
+        for j in range(2):
+            await_recv(by_chip.at[sweep, j, 0 : n_chip - 1], CHIPS + 2 * sweep + j)
+            g.append(-math.log2(total_tgt) - combine(by_chip.at[sweep, j]))
+        pot_tgt[...] = jnp.concatenate(g, axis=0)
     f_ref[...] = jnp.concatenate(f, axis=0) * (EPSILON / LOG2E)
-    g_ref[...] = g * (EPSILON / LOG2E)
+    g_ref[...] = jnp.concatenate(g, axis=0) * (EPSILON / LOG2E)
 
     for h in range(2):
         await_send(block_at(col, h), SRC_Z + h)
@@ -420,8 +429,9 @@
     for sweep in range(SWEEPS):
         for h in range(2):
             await_send(by_col.at[sweep, h, 0 : n_col - 1], ROWS + 2 * sweep + h)
-        await_send(by_pair.at[sweep, 0], PAIR + sweep)
-        await_send(by_chip.at[sweep, 0 : n_chip - 1], CHIPS + sweep)
+        for j in range(2):
+            await_send(by_pair.at[sweep, j, 0], PAIR + 2 * sweep + j)
+            await_send(by_chip.at[sweep, j, 0 : n_chip - 1], CHIPS + 2 * sweep + j)
 
 
 def solution(mesh):
@@ -463,8 +473,8 @@
                 pltpu.VMEM((rows, 128), F32),
                 pltpu.VMEM((rows, 128), F32),
                 pltpu.VMEM((SWEEPS, 2, n_col, rows // 256, 128), F32),
-                pltpu.VMEM((SWEEPS, 2, cols // 128, 128), F32),
-                pltpu.VMEM((SWEEPS, n_chip, cols // 128, 128), F32),
+                pltpu.VMEM((SWEEPS, 2, 2, cols // 256, 128), F32),
+                pltpu.VMEM((SWEEPS, 2, n_chip, cols // 256, 128), F32),
                 pltpu.SemaphoreType.DMA((SLOTS,)),
                 pltpu.SemaphoreType.DMA((SLOTS,)),
             ],

time: 92.1 us -> 91.4 us (level)
  no operation moved by 1% of the time
where the time goes in v6:
time: 91.4 us; the launch traced here: 91.2 us
  Pallas kernels  88 us (96%)
  local copies, waits for them, and re-layouts  2.59 us (3%)
    pallas_call x1, Pallas kernels, local(): pl.pallas_call(lambda *refs: kernel(n_row, n_col, *refs), out_shape=[jax....  88 us
    unnamed x2, local copies, waits for them, and re-layouts  2.59 us

profile of v6, /device:TPU:1, one launch (start us, length us, event | category | flops | bytes accessed | tf_op | source)
XLA Modules:
  0.0 91.2 jit_solution(2997127627351768174)
XLA Ops:
  0.6 88.0 %shard_map.59 = (f32[16,128]{1,0:T(8,128)}, f32[16,128]{1,0:T(8,128)}) custom-call(f32[16,2048]{1,0:T(8,128)} %refs_0_.1, f32[4,2048]{1,0:T(4,128)} %refs_1_.1, bf16[2048,2048]{1,0:T(8,128)(2,1)} %refs_2_.1, f32[16,128]{1,0:T(8,128)} %bitcast.3), custom_call_target="tpu_custom_call" | custom-call | tf_op jit(solution)/shard_map/pallas_call | solution.py:446
  88.6 1.3 %copy.8 = f32[2048]{0:T(1024)} copy(f32[2048]{0:T(1024)} %bitcast.5) | data formatting | bytes 16384
  89.9 1.3 %copy.9 = f32[2048]{0:T(1024)} copy(f32[2048]{0:T(1024)} %bitcast.4) | data formatting | bytes 16384

commit v7 on v6

--- a/solution.py
+++ b/solution.py
@@ -174,10 +174,23 @@
     half_peer = (row, half_col)
     z_near = [((y * 4 + lax.rem(depth + d, 4)) * 2 + core_id, col) for d in (1, 3)]
     y_peers = [((lax.rem(y + d, n_y) * 4 + depth) * 2 + core_id, col) for d in range(1, n_y)]
-    col_peers = [(row, lax.rem(col + d, n_col)) for d in range(1, n_col)]
-    chip_peers = [(lax.rem(chip + d, n_chip) * 2 + core_id, col) for d in range(1, n_chip)]
+    steps = sorted(
+        ((dx, dh) for dx in range(x_size) for dh in range(2)),
+        key=lambda d: -min(d[0], x_size - d[0]) - d[1],
+    )
+    sides = (plane_half, 1 - plane_half)
+    cols_by_hops = [sides[dh] * x_size + lax.rem(x_at + dx, x_size) for dx, dh in steps]
+    col_peers = [(row, c) for c in cols_by_hops[:-1]]
+    group_peers = [(r, c) for c in cols_by_hops[:-1] for r in (row, sib)] + [(sib, col)]
+    chip_steps = sorted(
+        ((dy, dz) for dy in range(n_y) for dz in range(4)),
+        key=lambda d: -min(d[0], n_y - d[0]) - 2 * min(d[1], 4 - d[1]),
+    )
+    chip_peers = [
+        ((lax.rem(y + dy, n_y) * 4 + lax.rem(depth + dz, 4)) * 2 + core_id, col)
+        for dy, dz in chip_steps[:-1]
+    ]
     pair_peer = (sib, col)
-    group_peers = col_peers + [(sib, lax.rem(col + d, n_col)) for d in range(n_col)]
 
     def put(source, target, index, peer):
         pltpu.make_async_remote_copy(
@@ -354,17 +367,19 @@
     n_strips = cols_here // 256
 
     def cost_of(n):
-        lanes = pl.ds(pl.multiple_of(n * 256, 256), 256)
+        lanes = pl.ds(pl.multiple_of(n * 512, 512), 512)
         cost[:, lanes] = jnp.dot(xt[...], us[:, lanes], preferred_element_type=F32)
 
     def cost_strip(n, carry):
         cost_of(n)
-        factor_strip(n + 1)
+        factor_strip(2 * n + 2)
+        factor_strip(2 * n + 3)
         return carry
 
     factor_strip(0)
-    lax.fori_loop(0, n_strips - 1, cost_strip, 0)
-    cost_of(n_strips - 1)
+    factor_strip(1)
+    lax.fori_loop(0, n_strips // 2 - 1, cost_strip, 0)
+    cost_of(n_strips // 2 - 1)
 
     n_part = half // 128
     n_lanes = cols_here // 2

time: 91.4 us -> 89.7 us (0.981)
  Pallas kernels: 88 us -> 86.2 us
    pallas_call x1, Pallas kernels: 88 us -> 86.2 us  [local(): pl.pallas_call(lambda *refs: kernel(n_row, n_col, *refs), out_shape=[jax....]
where the time goes in v7:
time: 89.7 us; the launch traced here: 89.4 us
  Pallas kernels  86.2 us (96%)
  local copies, waits for them, and re-layouts  2.59 us (3%)
    pallas_call x1, Pallas kernels, local(): pl.pallas_call(lambda *refs: kernel(n_row, n_col, *refs), out_shape=[jax....  86.2 us
    unnamed x2, local copies, waits for them, and re-layouts  2.59 us

profile of v7, /device:TPU:1, one launch (start us, length us, event | category | flops | bytes accessed | tf_op | source)
XLA Modules:
  0.0 89.4 jit_solution(5932815771747482536)
XLA Ops:
  0.6 86.2 %shard_map.59 = (f32[16,128]{1,0:T(8,128)}, f32[16,128]{1,0:T(8,128)}) custom-call(f32[16,2048]{1,0:T(8,128)} %refs_0_.1, f32[4,2048]{1,0:T(4,128)} %refs_1_.1, bf16[2048,2048]{1,0:T(8,128)(2,1)} %refs_2_.1, f32[16,128]{1,0:T(8,128)} %bitcast.3), custom_call_target="tpu_custom_call" | custom-call | tf_op jit(solution)/shard_map/pallas_call | solution.py:461
  86.8 1.3 %copy.8 = f32[2048]{0:T(1024)} copy(f32[2048]{0:T(1024)} %bitcast.5) | data formatting | bytes 16384
  88.1 1.3 %copy.9 = f32[2048]{0:T(1024)} copy(f32[2048]{0:T(1024)} %bitcast.4) | data formatting | bytes 16384
